TPU v7x, 256 devices: a whole 4x4x8 slice. The times are simulated.
256 devices in a mesh: dom: 32 (over z, x), orb: 8 (over y, core).
Axes of the slice: x: 4, y: 4, z: 8, core: 2. Of those that a mesh axis runs over, the one named last changes fastest.
Arguments:
- orbitals: float32 [16, 384, 64, 128], P('orb', 'dom'), may hold values from -400 to 400
- potential: float32 [384, 64, 128], P('dom'), may hold values from -8 to 8
Outputs:
- filtered_basis: float32 [16, 384, 64, 128], P('orb', 'dom')
All inputs are finite; a program needn't handle non-finite values.
Results may differ from a plain program's by a relative error of at most 0.0003.
Values sent between devices are 32-bit elements; how exact they have to be, the bound alone decides.
A program may use at most 64 MiB of HBM per device.

v0:
```python
import jax
import jax.numpy as jnp
from jax import lax
from jax.sharding import PartitionSpec as P

coefficients = (-49.0 / 18.0, 1.5, -0.15, 1.0 / 90.0)
spacing = 0.5
filter_centre = 23.0
filter_half = 23.0


def extended(block, sides, width):
    for axis, dim in sides:
        count = lax.axis_size(axis)
        forward = [(i, i + 1) for i in range(count - 1)]
        forward.append((count - 1, 0))
        backward = [(target, source) for source, target in forward]
        low = lax.ppermute(
            lax.slice_in_dim(block, block.shape[dim] - width, None, axis=dim), axis, forward
        )
        high = lax.ppermute(lax.slice_in_dim(block, 0, width, axis=dim), axis, backward)
        block = jnp.concatenate([low, block, high], axis=dim)
    return block


def hamiltonian(padded, row_count, near_potential, plane_margin):
    col_count = padded.shape[2] - 2 * plane_margin

    def portion(shift_rows, shift_cols):
        return padded[
            :,
            3 + shift_rows : 3 + shift_rows + row_count,
            plane_margin + shift_cols : plane_margin + shift_cols + col_count,
        ]

    centre_part = portion(0, 0)
    laplace = 3.0 * coefficients[0] * centre_part
    for offset in range(1, 4):
        laplace = laplace + coefficients[offset] * (portion(offset, 0) + portion(-offset, 0))
        laplace = laplace + coefficients[offset] * (
            jnp.roll(centre_part, offset, 2) + jnp.roll(centre_part, -offset, 2)
        )
        laplace = laplace + coefficients[offset] * (
            jnp.roll(centre_part, offset, 3) + jnp.roll(centre_part, -offset, 3)
        )
    return (-0.5 / (spacing * spacing) * laplace + near_potential * centre_part, centre_part)


def chain_steps(block, potential, extend, plane_margin):
    row_count = block.shape[1]

    def applied(vector):
        result, centre_part = hamiltonian(extend(vector), row_count, potential, plane_margin)
        return result

    first = (applied(block) - filter_centre * block) / filter_half
    second = 2.0 * (applied(first) - filter_centre * first) / filter_half - block
    third = 2.0 * (applied(second) - filter_centre * second) / filter_half - first
    return third


def orthonormal(flat, cell_total):
    local_gram = jnp.dot(
        flat, flat.T, precision=lax.Precision.HIGHEST, preferred_element_type=jnp.float32
    )
    gram = lax.psum(local_gram, ("dom", "orb")) / cell_total
    lower = jnp.linalg.cholesky(gram)
    return lax.linalg.triangular_solve(lower, flat, left_side=True, lower=True)


def regroup(block):
    return lax.all_to_all(block, "orb", split_axis=2, concat_axis=0, tiled=True)


def on_device(orbitals, potential):

    def extend_slab(vector):
        return extended(vector, (("dom", 1),), 3)

    filtered = chain_steps(orbitals, potential, extend_slab, 0)
    grouped = regroup(filtered)
    cell_total = (
        grouped.shape[1]
        * grouped.shape[2]
        * grouped.shape[3]
        * lax.axis_size("dom")
        * lax.axis_size("orb")
    )
    flat = grouped.reshape(grouped.shape[0], -1)
    basis = orthonormal(orthonormal(flat, cell_total), cell_total).reshape(grouped.shape)
    return lax.all_to_all(basis, "orb", split_axis=0, concat_axis=2, tiled=True)


def solution(mesh):
    return jax.shard_map(
        on_device,
        mesh=mesh,
        in_specs=(P("orb", "dom", None, None), P("dom", None, None)),
        out_specs=P("orb", "dom", None, None),
        check_vma=False,
    )
```

profile of v0, /device:TPU:1, one launch (start us, length us, event | category | flops | bytes accessed | tf_op | source)
XLA Modules:
  0.0 267.5 jit_solution(16394434240710894616)
XLA Ops:
  0.0 1.6 copy.14
  1.7 8.7 %collective-permute-start = (f32[2,3,64,128]{3,1,0,2:T(4,128)S(1)}, f32[2,3,64,128]{3,1,0,2:T(4,128)S(1)}, u32[]{:S(2)}, u32[]{:S(2)}) collective-permute-start(f32[2,3,64,128]{3,1,0,2:T(4,128)S(1)} %get-tuple-element.77), channel_id=1, source_target_pairs={{8,0},{16,8},{24,16},{32,24},{40,32},{48,40},{56,48},{64,56},{72,6... | collective-permute-start | bytes 589832 | tf_op jit(solution)/shard_map/ppermute | solution.py:21
  14.5 1.0 copy.46
  15.6 5.0 %collective-permute-done.1 = f32[2,3,64,128]{3,1,0,2:T(4,128)S(1)} collective-permute-done((f32[2,3,64,128]{3,1,0,2:T(4,128)S(1)}, f32[2,3,64,128]{3,1,0,2:T(4,128)S(1)}, u32[]{:S(2)}, u32[]{:S(2)}) %collective-permute-start.1) | collective-permute-done | bytes 196640 | tf_op jit(solution)/shard_map/ppermute | solution.py:18
  21.3 6.3 %broadcast_multiply_fusion = (f32[2,12,64,128]{3,1,0,2:T(8,128)S(1)}, f32[2,12,64,128]{3,1,0,2:T(8,128)S(1)}) fusion(f32[2,12,64,128]{3,1,0,2:T(8,128)S(1)} %copy.14, f32[12,64,128]{2,0,1:T(8,128)S(1)} %copy.43, f32[2,12,64,3]{3,1,0,2:T(8,128)S(1)} %get-tuple-element.84, f32[2,12,64,125]{3,1,0,2:T(8,128)S(1)} %get-tuple-element.86, ...), kind=kLoop, calls=%fused_computation.127 | loop fusion | flops 10223616 | bytes 12582912 | tf_op jit(solution)/shard_map/div | solution.py:56
  31.2 1.1 collective-permute-start.3
  32.3 4.5 %collective-permute-done.2 = f32[2,3,64,128]{3,1,0,2:T(4,128)S(1)} collective-permute-done((f32[2,3,64,128]{3,1,0,2:T(4,128)S(1)}, f32[2,3,64,128]{3,1,0,2:T(4,128)S(1)}, u32[]{:S(2)}, u32[]{:S(2)}) %collective-permute-start.2) | collective-permute-done | bytes 196640 | tf_op jit(solution)/shard_map/ppermute | solution.py:21
  36.7 3.8 %collective-permute-done.3 = f32[2,3,64,128]{3,1,0,2:T(4,128)S(1)} collective-permute-done((f32[2,3,64,128]{3,1,0,2:T(4,128)S(1)}, f32[2,3,64,128]{3,1,0,2:T(4,128)S(1)}, u32[]{:S(2)}, u32[]{:S(2)}) %collective-permute-start.3) | collective-permute-done | bytes 196640 | tf_op jit(solution)/shard_map/ppermute | solution.py:18
  41.2 6.7 %fusion.35 = f32[2,12,64,128]{3,1,0,2:T(8,128)S(1)} fusion(f32[2,12,64,128]{3,1,0,2:T(8,128)S(1)} %get-tuple-element.8, f32[2,3,64,128]{3,1,0,2:T(4,128)} %copy-done.5, f32[2,3,64,128]{3,1,0,2:T(4,128)} %copy-done.3, f32[2,12,64,128]{3,1,0,2:T(8,128)S(1)} %get-tuple-element.6, f32[2,12,63,128]{3,1,0,2:T(8,128)S(1)} %get-tuple-element.56, ...), kind=kLoop, calls=%fused_computation.48 | loop fusion | flops 10223616 | bytes 13369344 | tf_op jit(solution)/shard_map/sub | solution.py:57
  51.5 1.1 collective-permute-start.5
  52.6 3.8 %collective-permute-done.4 = f32[2,3,64,128]{3,1,0,2:T(4,128)S(1)} collective-permute-done((f32[2,3,64,128]{3,1,0,2:T(4,128)S(1)}, f32[2,3,64,128]{3,1,0,2:T(4,128)S(1)}, u32[]{:S(2)}, u32[]{:S(2)}) %collective-permute-start.4) | collective-permute-done | bytes 196640 | tf_op jit(solution)/shard_map/ppermute | solution.py:21
  56.4 3.7 %collective-permute-done.5 = f32[2,3,64,128]{3,1,0,2:T(4,128)S(1)} collective-permute-done((f32[2,3,64,128]{3,1,0,2:T(4,128)S(1)}, f32[2,3,64,128]{3,1,0,2:T(4,128)S(1)}, u32[]{:S(2)}, u32[]{:S(2)}) %collective-permute-start.5) | collective-permute-done | bytes 196640 | tf_op jit(solution)/shard_map/ppermute | solution.py:18
  60.8 6.5 %fusion.13 = f32[2,12,64,128]{3,1,0,2:T(8,128)S(1)} fusion(f32[2,3,64,128]{3,1,0,2:T(4,128)} %copy-done.6, f32[2,3,64,128]{3,1,0,2:T(4,128)} %copy-done.4, f32[2,12,64,128]{3,1,0,2:T(8,128)S(1)} %fusion.35, f32[2,12,63,128]{3,1,0,2:T(8,128)S(1)} %get-tuple-element.30, f32[2,12,1,128]{3,1,0,2:T(8,128)S(1)} %get-tuple-element.32, ...), kind=kLoop, calls=%fused_computation.26 | loop fusion | flops 10616832 | bytes 12582912 | tf_op jit(solution)/shard_map/sub | solution.py:58
  67.3 23.2 %all_to_all.33 = f32[2,12,64,128]{3,1,0,2:T(8,128)S(1)} all-to-all(f32[2,12,64,128]{3,1,0,2:T(8,128)S(1)} %fusion.13), channel_id=1, replica_groups=mesh['dom'=32,'orb'=8] {'orb'}, dimensions={2} | all-to-all | bytes 1572864 | tf_op jit(solution)/shard_map/all_to_all | solution.py:72
  91.2 1.1 fusion.137
  92.3 72.7 %psum.14 = f32[16,16]{0,1:T(8,128)S(1)} all-reduce(f32[16,16]{0,1:T(8,128)S(1)} %fusion.137), channel_id=1, replica_groups=mesh['dom'=32,'orb'=8] {'dom','orb'}, use_global_device_ids=true, to_apply=%region_0.1 | all-reduce | flops 256 | bytes 2048 | tf_op jit(solution)/shard_map/psum | solution.py:66
  165.1 1.5 cholesky.44
  167.9 1.2 custom-call.6
  169.9 1.1 fusion.138
  171.1 74.1 %psum.15 = f32[16,16]{0,1:T(8,128)S(1)} all-reduce(f32[16,16]{0,1:T(8,128)S(1)} %fusion.138), channel_id=1, replica_groups=mesh['dom'=32,'orb'=8] {'dom','orb'}, use_global_device_ids=true, to_apply=%region_3.6 | all-reduce | flops 256 | bytes 2048 | tf_op jit(solution)/shard_map/psum | solution.py:66
  245.3 1.5 cholesky.55
  248.1 1.2 custom-call.7
  250.3 16.2 %all_to_all.34 = f32[16,12,8,128]{3,2,1,0:T(8,128)S(1)} all-to-all(f32[16,12,8,128]{3,2,1,0:T(8,128)S(1)} %bitcast.42), channel_id=1, replica_groups=mesh['dom'=32,'orb'=8] {'orb'}, dimensions={0} | all-to-all | bytes 1572864 | tf_op jit(solution)/shard_map/all_to_all | solution.py:91
  266.5 1.0 copy.60
  (76 shorter events, 18.6 us)
Async XLA Ops:
  1.7 13.9 %collective-permute-start = (f32[2,3,64,128]{3,1,0,2:T(4,128)S(1)}, f32[2,3,64,128]{3,1,0,2:T(4,128)S(1)}, u32[]{:S(2)}, u32[]{:S(2)}) collective-permute-start(f32[2,3,64,128]{3,1,0,2:T(4,128)S(1)} %get-tuple-element.77), channel_id=1, source_target_pairs={{8,0},{16,8},{24,16},{32,24},{40,32},{48,40},{56,48},{64,56},{72,6... | collective-permute-start | bytes 589832 | tf_op jit(solution)/shard_map/ppermute | solution.py:21
  10.4 10.2 %collective-permute-start.1 = (f32[2,3,64,128]{3,1,0,2:T(4,128)S(1)}, f32[2,3,64,128]{3,1,0,2:T(4,128)S(1)}, u32[]{:S(2)}, u32[]{:S(2)}) collective-permute-start(f32[2,3,64,128]{3,1,0,2:T(4,128)S(1)} %get-tuple-element.78), channel_id=1, source_target_pairs={{0,8},{8,16},{16,24},{24,32},{32,40},{40,48},{48,56},{56,64},{64,7... | collective-permute-start | bytes 589832 | tf_op jit(solution)/shard_map/ppermute | solution.py:18
  13.2 1.0 copy-start
  15.6 5.0 %copy-start.1 = (f32[2,3,64,128]{3,1,0,2:T(4,128)}, f32[2,3,64,128]{3,1,0,2:T(4,128)S(1)}, u32[]{:S(2)}) copy-start(f32[2,3,64,128]{3,1,0,2:T(4,128)S(1)} %collective-permute-done) | copy-start | bytes 589828
  20.6 0.7 copy-start.2
  30.7 6.0 %collective-permute-start.2 = (f32[2,3,64,128]{3,1,0,2:T(4,128)S(1)}, f32[2,3,64,128]{3,1,0,2:T(4,128)S(1)}, u32[]{:S(2)}, u32[]{:S(2)}) collective-permute-start(f32[2,3,64,128]{3,1,0,2:T(4,128)S(1)} %get-tuple-element.59), channel_id=1, source_target_pairs={{8,0},{16,8},{24,16},{32,24},{40,32},{48,40},{56,48},{64,56},{72,6... | collective-permute-start | bytes 589832 | tf_op jit(solution)/shard_map/ppermute | solution.py:21
  31.2 9.3 %collective-permute-start.3 = (f32[2,3,64,128]{3,1,0,2:T(4,128)S(1)}, f32[2,3,64,128]{3,1,0,2:T(4,128)S(1)}, u32[]{:S(2)}, u32[]{:S(2)}) collective-permute-start(f32[2,3,64,128]{3,1,0,2:T(4,128)S(1)} %get-tuple-element.60), channel_id=1, source_target_pairs={{0,8},{8,16},{16,24},{24,32},{32,40},{40,48},{48,56},{56,64},{64,7... | collective-permute-start | bytes 589832 | tf_op jit(solution)/shard_map/ppermute | solution.py:18
  36.7 3.8 %copy-start.3 = (f32[2,3,64,128]{3,1,0,2:T(4,128)}, f32[2,3,64,128]{3,1,0,2:T(4,128)S(1)}, u32[]{:S(2)}) copy-start(f32[2,3,64,128]{3,1,0,2:T(4,128)S(1)} %collective-permute-done.2) | copy-start | bytes 589828
  40.5 0.7 copy-start.5
  51.1 5.3 %collective-permute-start.4 = (f32[2,3,64,128]{3,1,0,2:T(4,128)S(1)}, f32[2,3,64,128]{3,1,0,2:T(4,128)S(1)}, u32[]{:S(2)}, u32[]{:S(2)}) collective-permute-start(f32[2,3,64,128]{3,1,0,2:T(4,128)S(1)} %get-tuple-element.33), channel_id=1, source_target_pairs={{8,0},{16,8},{24,16},{32,24},{40,32},{48,40},{56,48},{64,56},{72,6... | collective-permute-start | bytes 589832 | tf_op jit(solution)/shard_map/ppermute | solution.py:21
  51.5 8.5 %collective-permute-start.5 = (f32[2,3,64,128]{3,1,0,2:T(4,128)S(1)}, f32[2,3,64,128]{3,1,0,2:T(4,128)S(1)}, u32[]{:S(2)}, u32[]{:S(2)}) collective-permute-start(f32[2,3,64,128]{3,1,0,2:T(4,128)S(1)} %get-tuple-element.34), channel_id=1, source_target_pairs={{0,8},{8,16},{16,24},{24,32},{32,40},{40,48},{48,56},{56,64},{64,7... | collective-permute-start | bytes 589832 | tf_op jit(solution)/shard_map/ppermute | solution.py:18
  56.4 3.7 %copy-start.4 = (f32[2,3,64,128]{3,1,0,2:T(4,128)}, f32[2,3,64,128]{3,1,0,2:T(4,128)S(1)}, u32[]{:S(2)}) copy-start(f32[2,3,64,128]{3,1,0,2:T(4,128)S(1)} %collective-permute-done.4) | copy-start | bytes 589828
  60.1 0.7 copy-start.6
where the time goes:
time: 268 us; the launch traced here: 267 us
  blocking collectives  186 us (69%)
  other arithmetic  27.5 us (10%)
  waiting for transfers between devices  20.7 us (8%)
  local copies, waits for them, and re-layouts  16.9 us (6%)
  starting transfers between devices  11.8 us (4%)
  matrix products  3.95 us (1%)
    psum x2, blocking collectives, orthonormal(): gram = lax.psum(local_gram, ('dom', 'orb')) / cell_total  147 us
    all_to_all x1, blocking collectives, regroup(): return lax.all_to_all(block, 'orb', split_axis=2, concat_axis=0, tiled=True)  23.2 us
    all_to_all x1, blocking collectives, on_device(): return lax.all_to_all(basis, 'orb', split_axis=0, concat_axis=2, tiled=True)  16.2 us
    ppermute x3, waiting for transfers between devices, extended(): lax.ppermute(lax.slice_in_dim(block, block.shape[dim] - width, None, axis...  12.4 us
    ppermute x3, starting transfers between devices, extended(): lax.ppermute(lax.slice_in_dim(block, 0, width, axis=dim), axis, backward)  9.61 us
    ppermute x3, waiting for transfers between devices, extended(): lax.ppermute(lax.slice_in_dim(block, 0, width, axis=dim), axis, backward)  8.22 us
    sub x1, other arithmetic, chain_steps(): 2.0 * (applied(first) - filter_centre * first) / filter_half - block  6.66 us
    sub x1, other arithmetic, chain_steps(): 2.0 * (applied(second) - filter_centre * second) / filter_half - first  6.54 us
  transfers between devices with their start and end apart: 6, of which 5 were waited for; matrix products, arithmetic and copies ran while one was open for 2% of the time, Pallas kernels for 0%

commit v1 on v0

v1 whole, which is shorter than its diff:
```python
import functools

import jax
import jax.numpy as jnp
from jax import lax
from jax.experimental import pallas as pl
from jax.experimental.pallas import tpu as pltpu
from jax.sharding import PartitionSpec as P

MESH = pl.DeviceIdType.MESH
F32 = jnp.float32
BF16 = jnp.bfloat16
coefficients = (-49.0 / 18.0, 1.5, -0.15, 1.0 / 90.0)
spacing = 0.5
filter_centre = 23.0
filter_half = 23.0
kinetic = -0.5 / (spacing * spacing) / filter_half
STEP = tuple(kinetic * c for c in coefficients)
DIAGONAL = 3.0 * STEP[0] - filter_centre / filter_half
PAD = 8


def split3(x):
    hi = x.astype(BF16)
    rest = x - hi.astype(F32)
    mid = rest.astype(BF16)
    low = (rest - mid.astype(F32)).astype(BF16)
    return hi, mid, low


def eliminate(gram, n):
    rows = lax.broadcasted_iota(jnp.int32, (n, 128), 0)
    lanes = lax.broadcasted_iota(jnp.int32, (n, 128), 1)
    work = jnp.where(lanes < n, gram, 0.0) + jnp.where(lanes == rows + n, 1.0, 0.0)
    for j in range(n - 1):
        column = jnp.broadcast_to(work[:, j : j + 1], (n, 128))
        pivot = jnp.broadcast_to(column[j : j + 1, :], (n, 128))
        row = jnp.broadcast_to(work[j : j + 1, :], (n, 128))
        factor = jnp.where(rows > j, column / pivot, 0.0)
        work = work - factor * row
    diagonal = jnp.sum(jnp.where(lanes == rows, work, 0.0), axis=1, keepdims=True)
    scaled = work / jnp.sqrt(jnp.broadcast_to(diagonal, (n, 128)))
    return jnp.where(lanes < n, pltpu.roll(scaled, 128 - n, 1), 0.0)


def kernel(
    sizes,
    orb_ref,
    pot_ref,
    out_ref,
    e0,
    e1,
    e2,
    diag,
    third,
    grouped,
    split_x,
    split_b,
    back,
    gram_orb,
    gram_dom,
    load_sem,
    halo_send,
    halo_recv,
    fwd_send,
    fwd_recv,
    fwd_own,
    gram_send,
    gram_recv,
    bck_send,
    bck_recv,
    bck_own,
):
    doms, orbs, own, layers, ny, nz, cells = sizes
    n = own * orbs
    chunk = ny // orbs
    half = layers - 6
    d = lax.axis_index("dom")
    o = lax.axis_index("orb")
    left = lax.rem(d + doms - 1, doms)
    right = lax.rem(d + 1, doms)

    barrier = pltpu.get_barrier_semaphore()

    @pl.loop(1, orbs)
    def _(p):
        pl.semaphore_signal(
            barrier, inc=1, device_id={"orb": lax.rem(o + p, orbs)}, device_id_type=MESH
        )

    @pl.loop(1, doms)
    def _(p):
        pl.semaphore_signal(
            barrier, inc=1, device_id={"dom": lax.rem(d + p, doms)}, device_id_type=MESH
        )

    loads = [pltpu.make_async_copy(pot_ref, diag, load_sem.at[0])]
    for a in range(own):
        loads.append(
            pltpu.make_async_copy(
                orb_ref.at[a], e0.at[a, pl.ds(3, layers), pl.ds(PAD, ny)], load_sem.at[1 + 3 * a]
            )
        )
        loads.append(
            pltpu.make_async_copy(
                orb_ref.at[a, :, pl.ds(ny - PAD, PAD)],
                e0.at[a, pl.ds(3, layers), pl.ds(0, PAD)],
                load_sem.at[2 + 3 * a],
            )
        )
        loads.append(
            pltpu.make_async_copy(
                orb_ref.at[a, :, pl.ds(0, PAD)],
                e0.at[a, pl.ds(3, layers), pl.ds(PAD + ny, PAD)],
                load_sem.at[3 + 3 * a],
            )
        )
    for copy in loads:
        copy.start()

    pl.semaphore_wait(barrier, orbs - 1 + doms - 1)

    fields = (e0, e1, e2)

    def halo(stage, a):
        dst = fields[stage]
        rows = pl.ds(PAD, ny)
        if stage == 0:
            low_src, high_src = orb_ref.at[a, pl.ds(0, 3)], orb_ref.at[a, pl.ds(layers - 3, 3)]
        else:
            low_src = dst.at[a, pl.ds(3, 3), rows]
            high_src = dst.at[a, pl.ds(layers, 3), rows]
        out = []
        for side, (src, at, to) in enumerate(((high_src, 0, right), (low_src, layers + 3, left))):
            out.append(
                pltpu.make_async_remote_copy(
                    src_ref=src,
                    dst_ref=dst.at[a, pl.ds(at, 3), rows],
                    send_sem=halo_send.at[stage, a, side],
                    recv_sem=halo_recv.at[stage, a, side],
                    device_id={"dom": to},
                    device_id_type=MESH,
                )
            )
        return out

    halos = [[halo(stage, a) for a in range(own)] for stage in range(3)]

    def apply_layer(stage, a, layer, slot):
        src = fields[stage]
        rows = pl.ds(PAD, ny)
        centre = src[a, layer + 3, rows, :]
        result = diag[layer] * centre
        for k in range(1, 4):
            near = src[a, layer + 3 + k, rows, :] + src[a, layer + 3 - k, rows, :]
            near = near + (
                src[a, layer + 3, pl.ds(PAD + k, ny), :] + src[a, layer + 3, pl.ds(PAD - k, ny), :]
            )
            near = near + (pltpu.roll(centre, k, 1) + pltpu.roll(centre, nz - k, 1))
            result = result + STEP[k] * near
        if stage > 0:
            result = 2.0 * result - fields[stage - 1][a, layer + 3, rows, :]
        if stage < 2:
            dst = fields[stage + 1]
            dst[a, layer + 3, rows, :] = result
            dst[a, layer + 3, pl.ds(0, PAD), :] = result[ny - PAD :, :]
            dst[a, layer + 3, pl.ds(PAD + ny, PAD), :] = result[:PAD, :]
        else:
            third[:, a, slot] = result.reshape(orbs, chunk, nz)

    def inner(stage, a):
        @pl.loop(0, half)
        def _(i):
            apply_layer(stage, a, i + 3, i)

    def outer(stage, a):
        @pl.loop(half, layers)
        def _(i):
            apply_layer(stage, a, lax.rem(i + 3, layers), i)

    def to_cells(a, part):
        at, count = (0, half) if part == 0 else (half, 6)

        @pl.loop(1, orbs)
        def _(p):
            to = lax.rem(o + p, orbs)
            pltpu.make_async_remote_copy(
                src_ref=third.at[to, a, pl.ds(at, count)],
                dst_ref=grouped.at[own * o + a, pl.ds(at, count)],
                send_sem=fwd_send.at[a, part],
                recv_sem=fwd_recv.at[a, part],
                device_id={"orb": to},
                device_id_type=MESH,
            ).start()

        pltpu.make_async_copy(
            third.at[o, a, pl.ds(at, count)],
            grouped.at[own * o + a, pl.ds(at, count)],
            fwd_own.at[a, part],
        ).start()

    def wait_cells(a, part):
        at, count = (0, half) if part == 0 else (half, 6)
        block = grouped.at[pl.ds(0, orbs - 1), pl.ds(at, count)]
        pltpu.make_async_copy(block, block, fwd_send.at[a, part]).wait()
        pltpu.make_async_copy(block, block, fwd_recv.at[a, part]).wait()
        single = grouped.at[0, pl.ds(at, count)]
        pltpu.make_async_copy(single, single, fwd_own.at[a, part]).wait()

    for a in range(own):
        for copy in halos[0][a]:
            copy.start()
    for copy in loads:
        copy.wait()

    @pl.loop(0, layers)
    def _(i):
        diag[i] = diag[i] * (1.0 / filter_half) + DIAGONAL

    for a in range(own):
        inner(0, a)
    for stage in range(3):
        for a in range(own):
            for copy in halos[stage][a]:
                copy.wait()
            outer(stage, a)
            if stage < 2:
                for copy in halos[stage + 1][a]:
                    copy.start()
                inner(stage + 1, a)
                if stage == 1:
                    to_cells(a, 0)
            else:
                to_cells(a, 1)

    flat = grouped.reshape(n * layers * chunk, nz)
    flat_back = back.reshape(n * layers * chunk, nz)
    stride = layers * chunk

    def split_slots(begin, end):
        @pl.loop(begin, end)
        def _(slot):
            for r in range(chunk):
                row = slot * chunk + r
                x = flat[pl.ds(row, n, stride=stride), :]
                lanes = pl.ds(pl.multiple_of(row * nz, nz), nz)
                for part, value in enumerate(split3(x)):
                    split_x[pl.ds(part * n, n), lanes] = value

    def gram_of(split, begin, end):
        x = split[:, begin * chunk * nz : end * chunk * nz]
        return lax.dot_general(x, x, (((1,), (1,)), ((), ())), preferred_element_type=F32)

    lane = lax.broadcasted_iota(jnp.int32, (8, 128), 1)

    def total(full, step):
        rows = full[0:n] + full[n : 2 * n] + full[2 * n : 3 * n]
        wide = jnp.concatenate([rows, jnp.zeros((n, 128 - 3 * n), F32)], axis=1)
        wide = wide + pltpu.roll(wide, 128 - n, 1) + pltpu.roll(wide, 128 - 2 * n, 1)
        packed = jnp.where(lane < n, wide[:8], pltpu.roll(wide[8:], n, 1))
        for axis, count, me, buf in (("orb", orbs, o, gram_orb), ("dom", doms, d, gram_dom)):
            which = 0 if axis == "orb" else 1
            buf[step, me] = packed

            @pl.loop(1, count)
            def _(p):
                pltpu.make_async_remote_copy(
                    src_ref=buf.at[step, me],
                    dst_ref=buf.at[step, me],
                    send_sem=gram_send.at[step, which],
                    recv_sem=gram_recv.at[step, which],
                    device_id={axis: lax.rem(me + p, count)},
                    device_id_type=MESH,
                ).start()

            block = buf.at[step, pl.ds(0, count - 1)]
            pltpu.make_async_copy(block, block, gram_send.at[step, which]).wait()
            pltpu.make_async_copy(block, block, gram_recv.at[step, which]).wait()
            packed = jnp.sum(buf[step], axis=0)
        packed = packed * (1.0 / cells)
        return jnp.concatenate([packed, pltpu.roll(packed, 128 - n, 1)], axis=0)

    def stacked(inverse):
        wide = inverse + pltpu.roll(inverse, n, 1) + pltpu.roll(inverse, 2 * n, 1)
        return jnp.concatenate(split3(wide), axis=0)[:, : 3 * n]

    def applied(weights, split, lanes):
        full = jnp.dot(weights, split[:, lanes], preferred_element_type=F32)
        return full[0:n] + (full[n : 2 * n] + full[2 * n : 3 * n])

    for a in range(own):
        wait_cells(a, 0)
    split_slots(0, half)
    full = gram_of(split_x, 0, half)
    for a in range(own):
        wait_cells(a, 1)
    split_slots(half, layers)
    full = full + gram_of(split_x, half, layers)

    weights_one = stacked(eliminate(total(full, 0), n))

    @pl.loop(0, layers)
    def _(slot):
        lanes = pl.ds(pl.multiple_of(slot * chunk * nz, chunk * nz), chunk * nz)
        for part, value in enumerate(split3(applied(weights_one, split_x, lanes))):
            split_b[pl.ds(part * n, n), lanes] = value

    weights_two = stacked(eliminate(total(gram_of(split_b, 0, layers), 1), n))

    def send_back(part, at, count, layer):
        @pl.loop(1, orbs)
        def _(p):
            to = lax.rem(o + p, orbs)
            pltpu.make_async_remote_copy(
                src_ref=back.at[pl.ds(own * to, own), pl.ds(at, count)],
                dst_ref=out_ref.at[:, pl.ds(layer, count), pl.ds(chunk * o, chunk)],
                send_sem=bck_send.at[part],
                recv_sem=bck_recv.at[part],
                device_id={"orb": to},
                device_id_type=MESH,
            ).start()

        pltpu.make_async_copy(
            back.at[pl.ds(own * o, own), pl.ds(at, count)],
            out_ref.at[:, pl.ds(layer, count), pl.ds(chunk * o, chunk)],
            bck_own.at[part],
        ).start()

    parts = ((0, half, 3), (half, 3, half + 3), (half + 3, 3, 0))
    for part, (at, count, layer) in enumerate(parts):

        @pl.loop(at, at + count)
        def _(slot):
            lanes = pl.ds(pl.multiple_of(slot * chunk * nz, chunk * nz), chunk * nz)
            y = applied(weights_two, split_b, lanes)
            for r in range(chunk):
                flat_back[pl.ds(slot * chunk + r, n, stride=stride), :] = y[:, r * nz : (r + 1) * nz]

        send_back(part, at, count, layer)
    for part, (at, count, layer) in enumerate(parts):
        block = back.at[pl.ds(0, own * (orbs - 1)), pl.ds(at, count)]
        pltpu.make_async_copy(block, block, bck_send.at[part]).wait()
        pltpu.make_async_copy(block, block, bck_recv.at[part]).wait()
        single = back.at[pl.ds(0, own), pl.ds(at, count)]
        pltpu.make_async_copy(single, single, bck_own.at[part]).wait()


def on_device(orbitals, potential):
    own, layers, ny, nz = orbitals.shape
    doms, orbs = lax.axis_size("dom"), lax.axis_size("orb")
    n = own * orbs
    chunk = ny // orbs
    cells = layers * doms * ny * nz
    width = layers * chunk * nz
    dma = pltpu.SemaphoreType.DMA
    field = pltpu.VMEM((own, layers + 6, ny + 2 * PAD, nz), F32)
    return pl.pallas_call(
        functools.partial(kernel, (doms, orbs, own, layers, ny, nz, cells)),
        out_shape=jax.ShapeDtypeStruct(orbitals.shape, F32),
        in_specs=[pl.BlockSpec(memory_space=pl.ANY)] * 2,
        out_specs=pl.BlockSpec(memory_space=pl.ANY),
        scratch_shapes=[
            field,
            field,
            field,
            pltpu.VMEM((layers, ny, nz), F32),
            pltpu.VMEM((orbs, own, layers, chunk, nz), F32),
            pltpu.VMEM((n, layers, chunk, nz), F32),
            pltpu.VMEM((3 * n, width), BF16),
            pltpu.VMEM((3 * n, width), BF16),
            pltpu.VMEM((n, layers, chunk, nz), F32),
            pltpu.VMEM((2, orbs, 8, 128), F32),
            pltpu.VMEM((2, doms, 8, 128), F32),
            dma((1 + 3 * own,)),
            dma((3, own, 2)),
            dma((3, own, 2)),
            dma((own, 2)),
            dma((own, 2)),
            dma((own, 2)),
            dma((2, 2)),
            dma((2, 2)),
            dma((3,)),
            dma((3,)),
            dma((3,)),
        ],
        compiler_params=pltpu.CompilerParams(
            collective_id=0, has_side_effects=True, vmem_limit_bytes=40 * 1024 * 1024
        ),
        cost_estimate=pl.CostEstimate(flops=100_000_000, bytes_accessed=4_000_000, transcendentals=0),
    )(orbitals, potential)


def solution(mesh):
    return jax.shard_map(
        on_device,
        mesh=mesh,
        in_specs=(P("orb", "dom", None, None), P("dom", None, None)),
        out_specs=P("orb", "dom", None, None),
        check_vma=False,
    )
```

time: 268 us -> 80.5 us (0.30)
  blocking collectives: 186 us -> 0 us
  Pallas kernels: 0 us -> 77.4 us
  other arithmetic: 27.5 us -> 0 us
  waiting for transfers between devices: 20.7 us -> 0 us
  local copies, waits for them, and re-layouts: 16.9 us -> 3.01 us
  starting transfers between devices: 11.8 us -> 0 us
  matrix products: 3.95 us -> 0 us
    psum x2 -> x0, blocking collectives: 147 us -> none  [orthonormal(): gram = lax.psum(local_gram, ('dom', 'orb')) / cell_total]
    pallas_call x0 -> x1, Pallas kernels: none -> 77.4 us  [on_device(): pl.pallas_call(functools.partial(kernel, (doms, orbs, own, layers, ny, nz...]
    all_to_all x2 -> x0, blocking collectives: 39.4 us -> none  [the longest x1 23.2 us: regroup(): return lax.all_to_all(block, 'orb', split_axis=2, concat_axis=0, tiled=True)]
    ppermute x6 -> x0, waiting for transfers between devices: 20.7 us -> none  [the longest x3 12.4 us: extended(): lax.ppermute(lax.slice_in_dim(block, block.shape[dim] - width, None, axis...]
    sub x2 -> x0, other arithmetic: 13.2 us -> none  [the longest x1 6.66 us: chain_steps(): 2.0 * (applied(first) - filter_centre * first) / filter_half - block]
    ppermute x6 -> x0, starting transfers between devices: 11.8 us -> none  [the longest x3 9.61 us: extended(): lax.ppermute(lax.slice_in_dim(block, 0, width, axis=dim), axis, backward)]
    slice x39 -> x0, local copies, waits for them, and re-layouts: 9.38 us -> none  [the longest x12 4.46 us: hamiltonian(): jnp.roll(centre_part, -offset, 3)]
    another operation x10 -> x0, other arithmetic: 8.01 us -> none  [the longest x6 4.26 us: orthonormal(): lower = jnp.linalg.cholesky(gram)]
  transfers between devices with their start and end apart: 6 -> 0, of which waited for: 5 -> 0; matrix products, arithmetic and copies ran while one was open for 2% -> 0% of each run, Pallas kernels for 0% -> 0%
where the time goes in v1:
time: 80.5 us; the launch traced here: 80.4 us
  Pallas kernels  77.4 us (96%)
  local copies, waits for them, and re-layouts  3.01 us (4%)
    pallas_call x1, Pallas kernels, on_device(): pl.pallas_call(functools.partial(kernel, (doms, orbs, own, layers, ny, nz...  77.4 us
    unnamed x5, local copies, waits for them, and re-layouts  3.01 us

profile of v1, /device:TPU:1, one launch (start us, length us, event | category | flops | bytes accessed | tf_op | source)
XLA Modules:
  0.0 80.4 jit_solution(15366338700751178299)
XLA Ops:
  0.0 0.0 copy-start
  0.0 1.1 %copy-done = f32[2,12,64,128]{3,2,1,0:T(8,128)S(1)} copy-done((f32[2,12,64,128]{3,2,1,0:T(8,128)S(1)}, f32[2,12,64,128]{3,2,1,0:T(8,128)}, u32[]{:S(2)}) %copy-start) | copy-done | bytes 786456
  1.1 0.0 copy-start.1
  1.1 1.0 %copy-done.1 = f32[12,64,128]{2,1,0:T(8,128)S(1)} copy-done((f32[12,64,128]{2,1,0:T(8,128)S(1)}, f32[12,64,128]{2,1,0:T(8,128)}, u32[]{:S(2)}) %copy-start.1) | copy-done | bytes 393240
  2.1 77.4 %shard_map.28 = f32[2,12,64,128]{3,2,1,0:T(8,128)S(1)} custom-call(f32[2,12,64,128]{3,2,1,0:T(8,128)S(1)} %copy-done, f32[12,64,128]{2,1,0:T(8,128)S(1)} %copy-done.1), custom_call_target="tpu_custom_call" | custom-call | flops 100000000 | bytes 4000000 | tf_op jit(solution)/shard_map/pallas_call | solution.py:357
  79.5 0.9 %copy.4 = f32[2,12,64,128]{3,2,1,0:T(8,128)} copy(f32[2,12,64,128]{3,2,1,0:T(8,128)S(1)} %shard_map.28) | data formatting | bytes 1572864
Async XLA Ops:
  0.0 1.1 %copy-start = (f32[2,12,64,128]{3,2,1,0:T(8,128)S(1)}, f32[2,12,64,128]{3,2,1,0:T(8,128)}, u32[]{:S(2)}) copy-start(f32[2,12,64,128]{3,2,1,0:T(8,128)} %orb_ref.1) | copy-start | bytes 2359300
  1.1 1.0 %copy-start.1 = (f32[12,64,128]{2,1,0:T(8,128)S(1)}, f32[12,64,128]{2,1,0:T(8,128)}, u32[]{:S(2)}) copy-start(f32[12,64,128]{2,1,0:T(8,128)} %pot_ref.1) | copy-start | bytes 1179652

commit v2 on v1

--- a/solution.py
+++ b/solution.py
@@ -18,6 +18,7 @@
 STEP = tuple(kinetic * c for c in coefficients)
 DIAGONAL = 3.0 * STEP[0] - filter_centre / filter_half
 PAD = 8
+LIMBS = 4
 
 
 def split3(x):
@@ -28,19 +29,94 @@
     return hi, mid, low
 
 
+def anchor_of(largest):
+    shift = largest * 2.0**23
+    return ((largest + shift) - shift) * (1.25 * 2.0**17)
+
+
+def limbs(x, anchor):
+    out = []
+    for part in range(LIMBS):
+        place = anchor * 2.0 ** (-8 * part)
+        value = (x + place) - place
+        x = x - value
+        out.append(value.astype(BF16))
+    return out
+
+
+def two_sum(a, b):
+    total = a + b
+    part = total - a
+    return total, (a - (total - part)) + (b - part)
+
+
+def add_pairs(a, b):
+    total, error = two_sum(a[0], b[0])
+    return total, error + (a[1] + b[1])
+
+
+def halves(x):
+    wide = x * 4097.0
+    high = wide - (wide - x)
+    return high, x - high
+
+
+def lane_of(x, j):
+    return jnp.broadcast_to(x[:, j : j + 1], x.shape)
+
+
+def row_of(x, j):
+    return jnp.broadcast_to(x[j : j + 1, :], x.shape)
+
+
+def product(left, right, n):
+    left_high, left_low = halves(left[0])
+    right_high, right_low = halves(right[0])
+    total, low = None, None
+    for k in range(n):
+        a, ah, al = lane_of(left[0], k), lane_of(left_high, k), lane_of(left_low, k)
+        b, bh, bl = row_of(right[0], k), row_of(right_high, k), row_of(right_low, k)
+        value = a * b
+        error = ((ah * bh - value) + ah * bl + al * bh) + al * bl
+        if right[1] is not None:
+            error = error + a * row_of(right[1], k)
+        if left[1] is not None:
+            error = error + lane_of(left[1], k) * b
+        if total is None:
+            total, low = value, error
+        else:
+            total, carry = two_sum(total, value)
+            low = low + (carry + error)
+    return total, low
+
+
 def eliminate(gram, n):
     rows = lax.broadcasted_iota(jnp.int32, (n, 128), 0)
     lanes = lax.broadcasted_iota(jnp.int32, (n, 128), 1)
     work = jnp.where(lanes < n, gram, 0.0) + jnp.where(lanes == rows + n, 1.0, 0.0)
     for j in range(n - 1):
-        column = jnp.broadcast_to(work[:, j : j + 1], (n, 128))
-        pivot = jnp.broadcast_to(column[j : j + 1, :], (n, 128))
-        row = jnp.broadcast_to(work[j : j + 1, :], (n, 128))
-        factor = jnp.where(rows > j, column / pivot, 0.0)
-        work = work - factor * row
+        column = lane_of(work, j)
+        factor = jnp.where(rows > j, column / row_of(column, j), 0.0)
+        work = work - factor * row_of(work, j)
     diagonal = jnp.sum(jnp.where(lanes == rows, work, 0.0), axis=1, keepdims=True)
     scaled = work / jnp.sqrt(jnp.broadcast_to(diagonal, (n, 128)))
     return jnp.where(lanes < n, pltpu.roll(scaled, 128 - n, 1), 0.0)
+
+
+def combined(gram, cells, n):
+    scale = 2.0**-20
+    high, low = gram[0] * scale, gram[1] * scale
+    rest = 1.0 / (cells * scale)
+    inverse_one = eliminate(high * rest, n)
+    turned = jnp.transpose(inverse_one)[:n]
+    turned = jnp.concatenate([turned, jnp.zeros((n, 128 - n), F32)], axis=1)
+    half = product((inverse_one, None), (high, low), n)
+    gram_two = product(half, (turned, None), n)
+    inverse_two = eliminate((gram_two[0] + gram_two[1]) * rest, n)
+    both = lane_of(inverse_two, 0) * row_of(inverse_one, 0)
+    for k in range(1, n):
+        both = both + lane_of(inverse_two, k) * row_of(inverse_one, k)
+    return both
 
 
 def kernel(
@@ -55,7 +131,6 @@
     third,
     grouped,
     split_x,
-    split_b,
     back,
     gram_orb,
     gram_dom,
@@ -169,12 +244,12 @@
             third[:, a, slot] = result.reshape(orbs, chunk, nz)
 
     def inner(stage, a):
-        @pl.loop(0, half)
+        @pl.loop(0, half, unroll=True)
         def _(i):
             apply_layer(stage, a, i + 3, i)
 
     def outer(stage, a):
-        @pl.loop(half, layers)
+        @pl.loop(half, layers, unroll=True)
         def _(i):
             apply_layer(stage, a, lax.rem(i + 3, layers), i)
 
@@ -238,74 +313,101 @@
     stride = layers * chunk
 
     def split_slots(begin, end):
-        @pl.loop(begin, end)
+        def larger(slot, most):
+            for r in range(chunk):
+                most = jnp.maximum(most, jnp.abs(flat[pl.ds(slot * chunk + r, n, stride=stride), :]))
+            return most
+
+        most = lax.fori_loop(begin, end, larger, jnp.zeros((n, nz), F32), unroll=2)
+        anchor = anchor_of(jnp.broadcast_to(jnp.max(most, axis=1, keepdims=True), (n, nz)))
+
+        @pl.loop(begin, end, unroll=2)
         def _(slot):
             for r in range(chunk):
                 row = slot * chunk + r
                 x = flat[pl.ds(row, n, stride=stride), :]
                 lanes = pl.ds(pl.multiple_of(row * nz, nz), nz)
-                for part, value in enumerate(split3(x)):
+                for part, value in enumerate(limbs(x, anchor)):
                     split_x[pl.ds(part * n, n), lanes] = value
 
-    def gram_of(split, begin, end):
-        x = split[:, begin * chunk * nz : end * chunk * nz]
-        return lax.dot_general(x, x, (((1,), (1,)), ((), ())), preferred_element_type=F32)
+    def gram_of(begin, end, pair):
+        for slot in range(begin, end):
+            x = split_x[:, slot * chunk * nz : (slot + 1) * chunk * nz]
+            value = lax.dot_general(x, x, (((1,), (1,)), ((), ())), preferred_element_type=F32)
+            if pair is None:
+                pair = value, jnp.zeros_like(value)
+            else:
+                high, error = two_sum(pair[0], value)
+                pair = high, pair[1] + error
+        return pair
 
     lane = lax.broadcasted_iota(jnp.int32, (8, 128), 1)
 
-    def total(full, step):
-        rows = full[0:n] + full[n : 2 * n] + full[2 * n : 3 * n]
-        wide = jnp.concatenate([rows, jnp.zeros((n, 128 - 3 * n), F32)], axis=1)
-        wide = wide + pltpu.roll(wide, 128 - n, 1) + pltpu.roll(wide, 128 - 2 * n, 1)
-        packed = jnp.where(lane < n, wide[:8], pltpu.roll(wide[8:], n, 1))
-        for axis, count, me, buf in (("orb", orbs, o, gram_orb), ("dom", doms, d, gram_dom)):
-            which = 0 if axis == "orb" else 1
-            buf[step, me] = packed
+    def total(pair):
+        parts = [tuple(v[p * n : (p + 1) * n] for v in pair) for p in range(LIMBS)]
+        low_first = add_pairs(add_pairs(parts[3], parts[2]), add_pairs(parts[1], parts[0]))
+        pad = jnp.zeros((n, 128 - LIMBS * n), F32)
+        wide = tuple(jnp.concatenate([v, pad], axis=1) for v in low_first)
+        for step in (2 * n, n):
+            wide = add_pairs(wide, tuple(pltpu.roll(v, 128 - step, 1) for v in wide))
+        top, bottom = tuple(v[:8] for v in wide), tuple(pltpu.roll(v[8:], n, 1) for v in wide)
+        high, low = (jnp.where(lane < n, t, b) for t, b in zip(top, bottom))
+        packed = jnp.where(lane < 2 * n, high, pltpu.roll(low, 2 * n, 1))
+        packed = jnp.where(lane < 4 * n, packed, 0.0)
+        for which, (axis, count, me, buf) in enumerate((("orb", orbs, o, gram_orb), ("dom", doms, d, gram_dom))):
+            buf[me] = packed
 
             @pl.loop(1, count)
             def _(p):
                 pltpu.make_async_remote_copy(
-                    src_ref=buf.at[step, me],
-                    dst_ref=buf.at[step, me],
-                    send_sem=gram_send.at[step, which],
-                    recv_sem=gram_recv.at[step, which],
+                    src_ref=buf.at[me],
+                    dst_ref=buf.at[me],
+                    send_sem=gram_send.at[which],
+                    recv_sem=gram_recv.at[which],
                     device_id={axis: lax.rem(me + p, count)},
                     device_id_type=MESH,
                 ).start()
 
-            block = buf.at[step, pl.ds(0, count - 1)]
-            pltpu.make_async_copy(block, block, gram_send.at[step, which]).wait()
-            pltpu.make_async_copy(block, block, gram_recv.at[step, which]).wait()
-            packed = jnp.sum(buf[step], axis=0)
-        packed = packed * (1.0 / cells)
-        return jnp.concatenate([packed, pltpu.roll(packed, 128 - n, 1)], axis=0)
-
-    def stacked(inverse):
-        wide = inverse + pltpu.roll(inverse, n, 1) + pltpu.roll(inverse, 2 * n, 1)
-        return jnp.concatenate(split3(wide), axis=0)[:, : 3 * n]
-
-    def applied(weights, split, lanes):
-        full = jnp.dot(weights, split[:, lanes], preferred_element_type=F32)
+            block = buf.at[pl.ds(0, count - 1)]
+            pltpu.make_async_copy(block, block, gram_recv.at[which]).wait()
+            value, error = buf[...], None
+            while count > 1:
+                count //= 2
+                value, extra = two_sum(value[:count], value[count:])
+                error = extra if error is None else extra + (error[:count] + error[count:])
+            packed = value[0] + jnp.where(lane >= 2 * n, pltpu.roll(error[0], 2 * n, 1), 0.0)
+            packed = jnp.where(lane < 4 * n, packed, 0.0)
+        low = pltpu.roll(packed, 128 - 2 * n, 1)
+        pair = tuple(
+            jnp.where(
+                lax.broadcasted_iota(jnp.int32, (n, 128), 1) < n,
+                jnp.concatenate([v, pltpu.roll(v, 128 - n, 1)], axis=0),
+                0.0,
+            )
+            for v in (packed, low)
+        )
+        return two_sum(pair[0], pair[1])
+
+    def stacked(matrix):
+        wide = matrix
+        for part in range(1, LIMBS):
+            wide = wide + pltpu.roll(matrix, part * n, 1)
+        return jnp.concatenate(split3(wide), axis=0)[:, : LIMBS * n]
+
+    def applied(weights, lanes):
+        full = jnp.dot(weights, split_x[:, lanes], preferred_element_type=F32)
         return full[0:n] + (full[n : 2 * n] + full[2 * n : 3 * n])
 
     for a in range(own):
         wait_cells(a, 0)
     split_slots(0, half)
-    full = gram_of(split_x, 0, half)
+    pair = gram_of(0, half, None)
     for a in range(own):
         wait_cells(a, 1)
     split_slots(half, layers)
-    full = full + gram_of(split_x, half, layers)
-
-    weights_one = stacked(eliminate(total(full, 0), n))
-
-    @pl.loop(0, layers)
-    def _(slot):
-        lanes = pl.ds(pl.multiple_of(slot * chunk * nz, chunk * nz), chunk * nz)
-        for part, value in enumerate(split3(applied(weights_one, split_x, lanes))):
-            split_b[pl.ds(part * n, n), lanes] = value
-
-    weights_two = stacked(eliminate(total(gram_of(split_b, 0, layers), 1), n))
+    pair = gram_of(half, layers, pair)
+    gram = total(pair)
+    weights = stacked(combined(gram, float(cells), n))
 
     def send_back(part, at, count, layer):
         @pl.loop(1, orbs)
@@ -332,7 +434,7 @@
         @pl.loop(at, at + count)
         def _(slot):
             lanes = pl.ds(pl.multiple_of(slot * chunk * nz, chunk * nz), chunk * nz)
-            y = applied(weights_two, split_b, lanes)
+            y = applied(weights, lanes)
             for r in range(chunk):
                 flat_back[pl.ds(slot * chunk + r, n, stride=stride), :] = y[:, r * nz : (r + 1) * nz]
 
@@ -343,6 +445,9 @@
         pltpu.make_async_copy(block, block, bck_recv.at[part]).wait()
         single = back.at[pl.ds(0, own), pl.ds(at, count)]
         pltpu.make_async_copy(single, single, bck_own.at[part]).wait()
+    for which, buf in enumerate((gram_orb, gram_dom)):
+        block = buf.at[pl.ds(0, (orbs, doms)[which] - 1)]
+        pltpu.make_async_copy(block, block, gram_send.at[which]).wait()
 
 
 def on_device(orbitals, potential):
@@ -366,25 +471,24 @@
             pltpu.VMEM((layers, ny, nz), F32),
             pltpu.VMEM((orbs, own, layers, chunk, nz), F32),
             pltpu.VMEM((n, layers, chunk, nz), F32),
-            pltpu.VMEM((3 * n, width), BF16),
-            pltpu.VMEM((3 * n, width), BF16),
+            pltpu.VMEM((LIMBS * n, width), BF16),
             pltpu.VMEM((n, layers, chunk, nz), F32),
-            pltpu.VMEM((2, orbs, 8, 128), F32),
-            pltpu.VMEM((2, doms, 8, 128), F32),
+            pltpu.VMEM((orbs, 8, 128), F32),
+            pltpu.VMEM((doms, 8, 128), F32),
             dma((1 + 3 * own,)),
             dma((3, own, 2)),
             dma((3, own, 2)),
             dma((own, 2)),
             dma((own, 2)),
             dma((own, 2)),
-            dma((2, 2)),
-            dma((2, 2)),
+            dma((2,)),
+            dma((2,)),
             dma((3,)),
             dma((3,)),
             dma((3,)),
         ],
         compiler_params=pltpu.CompilerParams(
-            collective_id=0, has_side_effects=True, vmem_limit_bytes=40 * 1024 * 1024
+            collective_id=0, has_side_effects=True, vmem_limit_bytes=60 * 1024 * 1024
         ),
         cost_estimate=pl.CostEstimate(flops=100_000_000, bytes_accessed=4_000_000, transcendentals=0),
     )(orbitals, potential)

time: 80.5 us -> 66.4 us (0.82)
  Pallas kernels: 77.4 us -> 64.2 us
  local copies, waits for them, and re-layouts: 3.01 us -> 2.09 us
    pallas_call x1, Pallas kernels: 77.4 us -> 64.2 us  [on_device(): pl.pallas_call(functools.partial(kernel, (doms, orbs, own, layers, ny, nz...]
    unnamed x5 -> x1, local copies, waits for them, and re-layouts: 3.01 us -> 2.09 us
where the time goes in v2:
time: 66.4 us; the launch traced here: 66.3 us
  Pallas kernels  64.2 us (97%)
  local copies, waits for them, and re-layouts  2.09 us (3%)
    pallas_call x1, Pallas kernels, on_device(): pl.pallas_call(functools.partial(kernel, (doms, orbs, own, layers, ny, nz...  64.2 us
    unnamed x1, local copies, waits for them, and re-layouts  2.09 us

profile of v2, /device:TPU:1, one launch (start us, length us, event | category | flops | bytes accessed | tf_op | source)
XLA Modules:
  0.0 66.3 jit_solution(5661672834955417959)
XLA Ops:
  0.0 64.2 %shard_map.28 = f32[2,12,64,128]{3,2,1,0:T(8,128)} custom-call(f32[2,12,64,128]{3,2,1,0:T(8,128)} %orb_ref.1, f32[12,64,128]{2,1,0:T(8,128)} %pot_ref.1), custom_call_target="tpu_custom_call" | custom-call | flops 100000000 | bytes 4000000 | tf_op jit(solution)/shard_map/pallas_call | solution.py:462
  64.2 2.1 %copy.4 = f32[2,12,64,128]{3,2,1,0:T(8,128)} copy(f32[2,12,64,128]{3,2,1,0:T(8,128)} %shard_map.28) | data formatting | bytes 1572864

commit v3 on v2

--- a/solution.py
+++ b/solution.py
@@ -17,7 +17,6 @@
 kinetic = -0.5 / (spacing * spacing) / filter_half
 STEP = tuple(kinetic * c for c in coefficients)
 DIAGONAL = 3.0 * STEP[0] - filter_centre / filter_half
-PAD = 8
 LIMBS = 4
 
 
@@ -127,6 +126,7 @@
     e0,
     e1,
     e2,
+    raw,
     diag,
     third,
     grouped,
@@ -137,6 +137,8 @@
     load_sem,
     halo_send,
     halo_recv,
+    pot_send,
+    pot_recv,
     fwd_send,
     fwd_recv,
     fwd_own,
@@ -169,27 +171,9 @@
             barrier, inc=1, device_id={"dom": lax.rem(d + p, doms)}, device_id_type=MESH
         )
 
-    loads = [pltpu.make_async_copy(pot_ref, diag, load_sem.at[0])]
+    loads = [pltpu.make_async_copy(pot_ref, raw.at[pl.ds(6, layers)], load_sem.at[0])]
     for a in range(own):
-        loads.append(
-            pltpu.make_async_copy(
-                orb_ref.at[a], e0.at[a, pl.ds(3, layers), pl.ds(PAD, ny)], load_sem.at[1 + 3 * a]
-            )
-        )
-        loads.append(
-            pltpu.make_async_copy(
-                orb_ref.at[a, :, pl.ds(ny - PAD, PAD)],
-                e0.at[a, pl.ds(3, layers), pl.ds(0, PAD)],
-                load_sem.at[2 + 3 * a],
-            )
-        )
-        loads.append(
-            pltpu.make_async_copy(
-                orb_ref.at[a, :, pl.ds(0, PAD)],
-                e0.at[a, pl.ds(3, layers), pl.ds(PAD + ny, PAD)],
-                load_sem.at[3 + 3 * a],
-            )
-        )
+        loads.append(pltpu.make_async_copy(orb_ref.at[a], e0.at[a, pl.ds(9, layers)], load_sem.at[1 + a]))
     for copy in loads:
         copy.start()
 
@@ -197,61 +181,94 @@
 
     fields = (e0, e1, e2)
 
-    def halo(stage, a):
-        dst = fields[stage]
-        rows = pl.ds(PAD, ny)
-        if stage == 0:
-            low_src, high_src = orb_ref.at[a, pl.ds(0, 3)], orb_ref.at[a, pl.ds(layers - 3, 3)]
-        else:
-            low_src = dst.at[a, pl.ds(3, 3), rows]
-            high_src = dst.at[a, pl.ds(layers, 3), rows]
+    def halo(piece, a):
         out = []
-        for side, (src, at, to) in enumerate(((high_src, 0, right), (low_src, layers + 3, left))):
+        for side, (at, to_at, to) in enumerate(
+            ((layers - 3 - 3 * piece, 6 - 3 * piece, right), (3 * piece, layers + 9 + 3 * piece, left))
+        ):
             out.append(
                 pltpu.make_async_remote_copy(
-                    src_ref=src,
-                    dst_ref=dst.at[a, pl.ds(at, 3), rows],
-                    send_sem=halo_send.at[stage, a, side],
-                    recv_sem=halo_recv.at[stage, a, side],
+                    src_ref=orb_ref.at[a, pl.ds(at, 3)],
+                    dst_ref=e0.at[a, pl.ds(to_at, 3)],
+                    send_sem=halo_send.at[a, piece, side],
+                    recv_sem=halo_recv.at[a, piece, side],
                     device_id={"dom": to},
                     device_id_type=MESH,
                 )
             )
         return out
 
-    halos = [[halo(stage, a) for a in range(own)] for stage in range(3)]
-
-    def apply_layer(stage, a, layer, slot):
+    odd = lax.rem(o, 2)
+    pair_device = o + 1 - 2 * odd
+
+    def margin_copies():
+        out = []
+        for side, (at, to_at, to) in enumerate(
+            ((layers - 3 - 3 * odd, 3 - 3 * odd, right), (3 * odd, layers + 6 + 3 * odd, left))
+        ):
+            taken = raw.at[pl.ds(to_at, 3)]
+            across = pltpu.make_async_remote_copy(
+                src_ref=pot_ref.at[pl.ds(at, 3)],
+                dst_ref=taken,
+                send_sem=pot_send.at[0, side],
+                recv_sem=pot_recv.at[0, side],
+                device_id={"dom": to},
+                device_id_type=MESH,
+            )
+            within = pltpu.make_async_remote_copy(
+                src_ref=taken,
+                dst_ref=taken,
+                send_sem=pot_send.at[1, side],
+                recv_sem=pot_recv.at[1, side],
+                device_id={"orb": pair_device},
+                device_id_type=MESH,
+            )
+            out.append((across, within))
+        return out
+
+    margins = margin_copies()
+
+    def start(copies):
+        for copy in copies:
+            copy.start()
+
+    def wait(copies):
+        for copy in copies:
+            copy.wait()
+
+    start(halo(0, 0))
+    start([across for across, _ in margins])
+    start(halo(1, 0))
+    start(halo(2, 0))
+    for a in range(1, own):
+        for piece in range(3):
+            start(halo(piece, a))
+
+    def apply_layer(stage, a, layer):
         src = fields[stage]
-        rows = pl.ds(PAD, ny)
-        centre = src[a, layer + 3, rows, :]
-        result = diag[layer] * centre
+        at = layer + 9 - 3 * stage
+        centre = src[a, at]
+        result = diag[layer + 6] * centre
         for k in range(1, 4):
-            near = src[a, layer + 3 + k, rows, :] + src[a, layer + 3 - k, rows, :]
-            near = near + (
-                src[a, layer + 3, pl.ds(PAD + k, ny), :] + src[a, layer + 3, pl.ds(PAD - k, ny), :]
-            )
+            near = src[a, at + k] + src[a, at - k]
+            near = near + (pltpu.roll(centre, k, 0) + pltpu.roll(centre, ny - k, 0))
             near = near + (pltpu.roll(centre, k, 1) + pltpu.roll(centre, nz - k, 1))
             result = result + STEP[k] * near
         if stage > 0:
-            result = 2.0 * result - fields[stage - 1][a, layer + 3, rows, :]
+            result = 2.0 * result - fields[stage - 1][a, at + 3]
         if stage < 2:
-            dst = fields[stage + 1]
-            dst[a, layer + 3, rows, :] = result
-            dst[a, layer + 3, pl.ds(0, PAD), :] = result[ny - PAD :, :]
-            dst[a, layer + 3, pl.ds(PAD + ny, PAD), :] = result[:PAD, :]
+            fields[stage + 1][a, at - 3] = result
         else:
-            third[:, a, slot] = result.reshape(orbs, chunk, nz)
-
-    def inner(stage, a):
-        @pl.loop(0, half, unroll=True)
-        def _(i):
-            apply_layer(stage, a, i + 3, i)
-
-    def outer(stage, a):
-        @pl.loop(half, layers, unroll=True)
-        def _(i):
-            apply_layer(stage, a, lax.rem(i + 3, layers), i)
+            third[:, a, (layer - 3) % layers] = result.reshape(orbs, chunk, nz)
+
+    inner = range(3, layers - 3)
+
+    def margin(step):
+        return (*range(-3 * step, 3 - 3 * step), *range(layers - 3 + 3 * step, layers + 3 * step))
+
+    def apply_layers(stage, a, chosen):
+        for layer in chosen:
+            apply_layer(stage, a, layer)
 
     def to_cells(a, part):
         at, count = (0, half) if part == 0 else (half, 6)
@@ -277,36 +294,49 @@
     def wait_cells(a, part):
         at, count = (0, half) if part == 0 else (half, 6)
         block = grouped.at[pl.ds(0, orbs - 1), pl.ds(at, count)]
-        pltpu.make_async_copy(block, block, fwd_send.at[a, part]).wait()
         pltpu.make_async_copy(block, block, fwd_recv.at[a, part]).wait()
         single = grouped.at[0, pl.ds(at, count)]
         pltpu.make_async_copy(single, single, fwd_own.at[a, part]).wait()
 
-    for a in range(own):
-        for copy in halos[0][a]:
-            copy.start()
-    for copy in loads:
-        copy.wait()
-
-    @pl.loop(0, layers)
-    def _(i):
-        diag[i] = diag[i] * (1.0 / filter_half) + DIAGONAL
-
-    for a in range(own):
-        inner(0, a)
-    for stage in range(3):
-        for a in range(own):
-            for copy in halos[stage][a]:
-                copy.wait()
-            outer(stage, a)
-            if stage < 2:
-                for copy in halos[stage + 1][a]:
-                    copy.start()
-                inner(stage + 1, a)
-                if stage == 1:
-                    to_cells(a, 0)
-            else:
-                to_cells(a, 1)
+    def weigh(begin, end):
+        @pl.loop(begin, end)
+        def _(i):
+            diag[i] = raw[i] * (1.0 / filter_half) + DIAGONAL
+
+    wait(loads)
+    weigh(6, layers + 6)
+    apply_layers(0, 0, inner)
+    wait(halo(0, 0))
+    apply_layers(0, 0, margin(0))
+    apply_layers(1, 0, inner)
+    for across, _ in margins:
+        across.wait()
+    for _, within in margins:
+        within.start()
+    for _, within in margins:
+        within.wait()
+    weigh(0, 6)
+    weigh(layers + 6, layers + 12)
+
+    def rest(a):
+        wait(halo(1, a))
+        apply_layers(0, a, margin(1))
+        apply_layers(1, a, margin(0))
+        apply_layers(2, a, inner)
+        to_cells(a, 0)
+        wait(halo(2, a))
+        apply_layers(0, a, margin(2))
+        apply_layers(1, a, margin(1))
+        apply_layers(2, a, margin(0))
+        to_cells(a, 1)
+
+    rest(0)
+    for a in range(1, own):
+        apply_layers(0, a, inner)
+        wait(halo(0, a))
+        apply_layers(0, a, margin(0))
+        apply_layers(1, a, inner)
+        rest(a)
 
     flat = grouped.reshape(n * layers * chunk, nz)
     flat_back = back.reshape(n * layers * chunk, nz)
@@ -342,6 +372,8 @@
         return pair
 
     lane = lax.broadcasted_iota(jnp.int32, (8, 128), 1)
+    lane4 = lax.broadcasted_iota(jnp.int32, (4, 128), 1)
+    lows = (lane4 & 32) == 32
 
     def total(pair):
         parts = [tuple(v[p * n : (p + 1) * n] for v in pair) for p in range(LIMBS)]
@@ -353,7 +385,7 @@
         top, bottom = tuple(v[:8] for v in wide), tuple(pltpu.roll(v[8:], n, 1) for v in wide)
         high, low = (jnp.where(lane < n, t, b) for t, b in zip(top, bottom))
         packed = jnp.where(lane < 2 * n, high, pltpu.roll(low, 2 * n, 1))
-        packed = jnp.where(lane < 4 * n, packed, 0.0)
+        packed = jnp.where(lane4 < 64, packed[:4], pltpu.roll(packed, 64, 1)[4:])
         for which, (axis, count, me, buf) in enumerate((("orb", orbs, o, gram_orb), ("dom", doms, d, gram_dom))):
             buf[me] = packed
 
@@ -375,8 +407,8 @@
                 count //= 2
                 value, extra = two_sum(value[:count], value[count:])
                 error = extra if error is None else extra + (error[:count] + error[count:])
-            packed = value[0] + jnp.where(lane >= 2 * n, pltpu.roll(error[0], 2 * n, 1), 0.0)
-            packed = jnp.where(lane < 4 * n, packed, 0.0)
+            packed = value[0] + jnp.where(lows, pltpu.roll(error[0], 2 * n, 1), 0.0)
+        packed = jnp.concatenate([packed, pltpu.roll(packed, 64, 1)], axis=0)
         low = pltpu.roll(packed, 128 - 2 * n, 1)
         pair = tuple(
             jnp.where(
@@ -445,6 +477,10 @@
         pltpu.make_async_copy(block, block, bck_recv.at[part]).wait()
         single = back.at[pl.ds(0, own), pl.ds(at, count)]
         pltpu.make_async_copy(single, single, bck_own.at[part]).wait()
+    for a in range(own):
+        for part, (at, count) in enumerate(((0, half), (half, 6))):
+            block = grouped.at[pl.ds(0, orbs - 1), pl.ds(at, count)]
+            pltpu.make_async_copy(block, block, fwd_send.at[a, part]).wait()
     for which, buf in enumerate((gram_orb, gram_dom)):
         block = buf.at[pl.ds(0, (orbs, doms)[which] - 1)]
         pltpu.make_async_copy(block, block, gram_send.at[which]).wait()
@@ -458,26 +494,32 @@
     cells = layers * doms * ny * nz
     width = layers * chunk * nz
     dma = pltpu.SemaphoreType.DMA
-    field = pltpu.VMEM((own, layers + 6, ny + 2 * PAD, nz), F32)
+
+    def field(extra):
+        return pltpu.VMEM((own, layers + extra, ny, nz), F32)
+
     return pl.pallas_call(
         functools.partial(kernel, (doms, orbs, own, layers, ny, nz, cells)),
-        out_shape=jax.ShapeDtypeStruct(orbitals.shape, F32),
-        in_specs=[pl.BlockSpec(memory_space=pl.ANY)] * 2,
-        out_specs=pl.BlockSpec(memory_space=pl.ANY),
+        out_shape=pltpu.VMEM(orbitals.shape, F32),
+        in_specs=[pl.BlockSpec(memory_space=pltpu.HBM)] * 2,
+        out_specs=pl.BlockSpec(memory_space=pltpu.VMEM),
         scratch_shapes=[
-            field,
-            field,
-            field,
-            pltpu.VMEM((layers, ny, nz), F32),
+            field(18),
+            field(12),
+            field(6),
+            pltpu.VMEM((layers + 12, ny, nz), F32),
+            pltpu.VMEM((layers + 12, ny, nz), F32),
             pltpu.VMEM((orbs, own, layers, chunk, nz), F32),
             pltpu.VMEM((n, layers, chunk, nz), F32),
             pltpu.VMEM((LIMBS * n, width), BF16),
             pltpu.VMEM((n, layers, chunk, nz), F32),
-            pltpu.VMEM((orbs, 8, 128), F32),
-            pltpu.VMEM((doms, 8, 128), F32),
-            dma((1 + 3 * own,)),
-            dma((3, own, 2)),
-            dma((3, own, 2)),
+            pltpu.VMEM((orbs, 4, 128), F32),
+            pltpu.VMEM((doms, 4, 128), F32),
+            dma((1 + own,)),
+            dma((own, 3, 2)),
+            dma((own, 3, 2)),
+            dma((2, 2)),
+            dma((2, 2)),
             dma((own, 2)),
             dma((own, 2)),
             dma((own, 2)),
@@ -488,10 +530,10 @@
             dma((3,)),
         ],
         compiler_params=pltpu.CompilerParams(
-            collective_id=0, has_side_effects=True, vmem_limit_bytes=60 * 1024 * 1024
+            collective_id=0, has_side_effects=True, vmem_limit_bytes=40 * 1024 * 1024
         ),
         cost_estimate=pl.CostEstimate(flops=100_000_000, bytes_accessed=4_000_000, transcendentals=0),
-    )(orbitals, potential)
+    )(*(pltpu.with_memory_space_constraint(v, pltpu.HBM) for v in (orbitals, potential)))
 
 
 def solution(mesh):

time: 66.4 us -> 62.5 us (0.941)
  Pallas kernels: 64.2 us -> 61.6 us
  local copies, waits for them, and re-layouts: 2.09 us -> 0.88 us
    pallas_call x1, Pallas kernels: 64.2 us -> 61.6 us  [on_device(): pl.pallas_call(functools.partial(kernel, (doms, orbs, own, layers, ny, nz...]
    unnamed x1, local copies, waits for them, and re-layouts: 2.09 us -> 0.88 us
where the time goes in v3:
time: 62.5 us
  Pallas kernels  61.6 us (99%)
  local copies, waits for them, and re-layouts  0.88 us (1%)
    pallas_call x1, Pallas kernels, on_device(): pl.pallas_call(functools.partial(kernel, (doms, orbs, own, layers, ny, nz...  61.6 us

profile of v3, /device:TPU:1, one launch (start us, length us, event | category | flops | bytes accessed | tf_op | source)
XLA Modules:
  0.0 62.5 jit_solution(3878375559631838285)
XLA Ops:
  0.0 61.6 %shard_map.28 = f32[2,12,64,128]{3,2,1,0:T(8,128)S(1)} custom-call(f32[2,12,64,128]{3,2,1,0:T(8,128)} %orb_ref.1, f32[12,64,128]{2,1,0:T(8,128)} %pot_ref.1), custom_call_target="tpu_custom_call" | custom-call | flops 100000000 | bytes 4000000 | tf_op jit(solution)/shard_map/pallas_call | solution.py:501
  61.6 0.9 %copy.4 = f32[2,12,64,128]{3,2,1,0:T(8,128)} copy(f32[2,12,64,128]{3,2,1,0:T(8,128)S(1)} %shard_map.28) | data formatting | bytes 1572864

commit v4 on v3

--- a/solution.py
+++ b/solution.py
@@ -93,10 +93,16 @@
     rows = lax.broadcasted_iota(jnp.int32, (n, 128), 0)
     lanes = lax.broadcasted_iota(jnp.int32, (n, 128), 1)
     work = jnp.where(lanes < n, gram, 0.0) + jnp.where(lanes == rows + n, 1.0, 0.0)
-    for j in range(n - 1):
-        column = lane_of(work, j)
-        factor = jnp.where(rows > j, column / row_of(column, j), 0.0)
-        work = work - factor * row_of(work, j)
+    for j in range(0, n, 2):
+        first, second = lane_of(work, j), lane_of(work, j + 1)
+        row, next_row = row_of(work, j), row_of(work, j + 1)
+        a, b, c, d = row_of(first, j), row_of(second, j), row_of(first, j + 1), row_of(second, j + 1)
+        over = 1.0 / a
+        over_next = a / (a * d - b * c)
+        factor = first * over
+        next_factor = jnp.where(rows > j + 1, (second - factor * b) * over_next, 0.0)
+        next_row = next_row - (c * over) * row
+        work = work - jnp.where(rows > j, factor, 0.0) * row - next_factor * next_row
     diagonal = jnp.sum(jnp.where(lanes == rows, work, 0.0), axis=1, keepdims=True)
     scaled = work / jnp.sqrt(jnp.broadcast_to(diagonal, (n, 128)))
     return jnp.where(lanes < n, pltpu.roll(scaled, 128 - n, 1), 0.0)
@@ -141,7 +147,6 @@
     pot_recv,
     fwd_send,
     fwd_recv,
-    fwd_own,
     gram_send,
     gram_recv,
     bck_send,
@@ -181,52 +186,55 @@
 
     fields = (e0, e1, e2)
 
-    def halo(piece, a):
+    def halo(a, begin, end):
         out = []
         for side, (at, to_at, to) in enumerate(
-            ((layers - 3 - 3 * piece, 6 - 3 * piece, right), (3 * piece, layers + 9 + 3 * piece, left))
+            ((layers - end, 9 - end, right), (begin, layers + 9 + begin, left))
         ):
             out.append(
                 pltpu.make_async_remote_copy(
-                    src_ref=orb_ref.at[a, pl.ds(at, 3)],
-                    dst_ref=e0.at[a, pl.ds(to_at, 3)],
-                    send_sem=halo_send.at[a, piece, side],
-                    recv_sem=halo_recv.at[a, piece, side],
+                    src_ref=orb_ref.at[a, pl.ds(at, end - begin)],
+                    dst_ref=e0.at[a, pl.ds(to_at, end - begin)],
+                    send_sem=halo_send.at[a, begin // 3 + begin // 8, side],
+                    recv_sem=halo_recv.at[a, begin // 3 + begin // 8, side],
                     device_id={"dom": to},
                     device_id_type=MESH,
                 )
             )
         return out
 
-    odd = lax.rem(o, 2)
-    pair_device = o + 1 - 2 * odd
-
-    def margin_copies():
-        out = []
-        for side, (at, to_at, to) in enumerate(
-            ((layers - 3 - 3 * odd, 3 - 3 * odd, right), (3 * odd, layers + 6 + 3 * odd, left))
-        ):
-            taken = raw.at[pl.ds(to_at, 3)]
-            across = pltpu.make_async_remote_copy(
-                src_ref=pot_ref.at[pl.ds(at, 3)],
-                dst_ref=taken,
+    mine = pl.ds(chunk * o, chunk)
+    across = []
+    for side, (at, to_at, to) in enumerate(((layers - 6, 0, right), (0, layers + 6, left))):
+        across.append(
+            pltpu.make_async_remote_copy(
+                src_ref=pot_ref.at[pl.ds(at, 6), mine],
+                dst_ref=raw.at[pl.ds(to_at, 6), mine],
                 send_sem=pot_send.at[0, side],
                 recv_sem=pot_recv.at[0, side],
                 device_id={"dom": to},
                 device_id_type=MESH,
             )
-            within = pltpu.make_async_remote_copy(
-                src_ref=taken,
-                dst_ref=taken,
-                send_sem=pot_send.at[1, side],
-                recv_sem=pot_recv.at[1, side],
-                device_id={"orb": pair_device},
-                device_id_type=MESH,
-            )
-            out.append((across, within))
-        return out
-
-    margins = margin_copies()
+        )
+
+    def share_margins():
+        for side, at in enumerate((0, layers + 6)):
+
+            @pl.loop(1, orbs)
+            def _(p):
+                pltpu.make_async_remote_copy(
+                    src_ref=raw.at[pl.ds(at, 6), mine],
+                    dst_ref=raw.at[pl.ds(at, 6), mine],
+                    send_sem=pot_send.at[1, side],
+                    recv_sem=pot_recv.at[1, side],
+                    device_id={"orb": lax.rem(o + p, orbs)},
+                    device_id_type=MESH,
+                ).start()
+
+    def wait_margins(sems):
+        for side in range(2):
+            block = raw.at[pl.ds(0, 6), pl.ds(0, ny - chunk)]
+            pltpu.make_async_copy(block, block, sems.at[1, side]).wait()
 
     def start(copies):
         for copy in copies:
@@ -236,13 +244,12 @@
         for copy in copies:
             copy.wait()
 
-    start(halo(0, 0))
-    start([across for across, _ in margins])
-    start(halo(1, 0))
-    start(halo(2, 0))
-    for a in range(1, own):
-        for piece in range(3):
-            start(halo(piece, a))
+    reach = [(0, 3), (3, 6), (6, 9)]
+    pieces = [reach] * (own - 1) + [reach[:2] + [(6, 8), (8, 9)]]
+    start(across)
+    for a in range(own):
+        for begin, end in pieces[a]:
+            start(halo(a, begin, end))
 
     def apply_layer(stage, a, layer):
         src = fields[stage]
@@ -263,40 +270,37 @@
 
     inner = range(3, layers - 3)
 
-    def margin(step):
-        return (*range(-3 * step, 3 - 3 * step), *range(layers - 3 + 3 * step, layers + 3 * step))
-
-    def apply_layers(stage, a, chosen):
-        for layer in chosen:
+    def newly(stage, a, begin, end):
+        low, high = 3 * (stage + 1), layers - 3 * (stage + 1)
+        for layer in (*range(low - end, low - begin), *range(high + begin, high + end)):
             apply_layer(stage, a, layer)
 
-    def to_cells(a, part):
-        at, count = (0, half) if part == 0 else (half, 6)
-
-        @pl.loop(1, orbs)
-        def _(p):
-            to = lax.rem(o + p, orbs)
-            pltpu.make_async_remote_copy(
-                src_ref=third.at[to, a, pl.ds(at, count)],
-                dst_ref=grouped.at[own * o + a, pl.ds(at, count)],
-                send_sem=fwd_send.at[a, part],
-                recv_sem=fwd_recv.at[a, part],
-                device_id={"orb": to},
-                device_id_type=MESH,
-            ).start()
-
-        pltpu.make_async_copy(
-            third.at[o, a, pl.ds(at, count)],
-            grouped.at[own * o + a, pl.ds(at, count)],
-            fwd_own.at[a, part],
-        ).start()
-
-    def wait_cells(a, part):
-        at, count = (0, half) if part == 0 else (half, 6)
-        block = grouped.at[pl.ds(0, orbs - 1), pl.ds(at, count)]
-        pltpu.make_async_copy(block, block, fwd_recv.at[a, part]).wait()
-        single = grouped.at[0, pl.ds(at, count)]
-        pltpu.make_async_copy(single, single, fwd_own.at[a, part]).wait()
+    slots_of = {(3, 6): ((0, half),), (6, 9): ((half, 6),), (6, 8): ((half, 2), (half + 4, 2)), (8, 9): ((half + 2, 2),)}
+
+    def to_cells(a, piece):
+        part = pieces[a].index(piece) - 1
+        for at, count in slots_of[piece]:
+
+            @pl.loop(1, orbs)
+            def _(p):
+                to = lax.rem(o + p, orbs)
+                pltpu.make_async_remote_copy(
+                    src_ref=third.at[to, a, pl.ds(at, count)],
+                    dst_ref=grouped.at[own * o + a, pl.ds(at, count)],
+                    send_sem=fwd_send.at[a, part],
+                    recv_sem=fwd_recv.at[a, part],
+                    device_id={"orb": to},
+                    device_id_type=MESH,
+                ).start()
+
+        for at, count in slots_of[piece]:
+            for slot in range(at, at + count):
+                grouped[own * o + a, slot] = third[o, a, slot]
+
+    def wait_cells(a, part, sems):
+        count = sum(count for _, count in slots_of[pieces[a][part + 1]])
+        block = grouped.at[pl.ds(0, orbs - 1), pl.ds(0, count)]
+        pltpu.make_async_copy(block, block, sems.at[a, part]).wait()
 
     def weigh(begin, end):
         @pl.loop(begin, end)
@@ -305,63 +309,55 @@
 
     wait(loads)
     weigh(6, layers + 6)
-    apply_layers(0, 0, inner)
-    wait(halo(0, 0))
-    apply_layers(0, 0, margin(0))
-    apply_layers(1, 0, inner)
-    for across, _ in margins:
-        across.wait()
-    for _, within in margins:
-        within.start()
-    for _, within in margins:
-        within.wait()
-    weigh(0, 6)
-    weigh(layers + 6, layers + 12)
-
-    def rest(a):
-        wait(halo(1, a))
-        apply_layers(0, a, margin(1))
-        apply_layers(1, a, margin(0))
-        apply_layers(2, a, inner)
-        to_cells(a, 0)
-        wait(halo(2, a))
-        apply_layers(0, a, margin(2))
-        apply_layers(1, a, margin(1))
-        apply_layers(2, a, margin(0))
-        to_cells(a, 1)
-
-    rest(0)
-    for a in range(1, own):
-        apply_layers(0, a, inner)
-        wait(halo(0, a))
-        apply_layers(0, a, margin(0))
-        apply_layers(1, a, inner)
-        rest(a)
+    for layer in inner:
+        apply_layer(0, 0, layer)
+    for copy in across:
+        copy.wait()
+    share_margins()
+    for a in range(own):
+        if a > 0:
+            for layer in inner:
+                apply_layer(0, a, layer)
+        for begin, end in pieces[a]:
+            wait(halo(a, begin, end))
+            if a == 0 and begin == 3:
+                wait_margins(pot_recv)
+                weigh(0, 6)
+                weigh(layers + 6, layers + 12)
+            newly(0, a, begin, end)
+            newly(1, a, begin, end)
+            if begin > 0:
+                newly(2, a, begin, end)
+                to_cells(a, (begin, end))
 
     flat = grouped.reshape(n * layers * chunk, nz)
     flat_back = back.reshape(n * layers * chunk, nz)
     stride = layers * chunk
 
-    def split_slots(begin, end):
+    def split_slots(ranges):
         def larger(slot, most):
             for r in range(chunk):
                 most = jnp.maximum(most, jnp.abs(flat[pl.ds(slot * chunk + r, n, stride=stride), :]))
             return most
 
-        most = lax.fori_loop(begin, end, larger, jnp.zeros((n, nz), F32), unroll=2)
+        most = jnp.zeros((n, nz), F32)
+        for at, count in ranges:
+            most = lax.fori_loop(at, at + count, larger, most, unroll=2)
         anchor = anchor_of(jnp.broadcast_to(jnp.max(most, axis=1, keepdims=True), (n, nz)))
 
-        @pl.loop(begin, end, unroll=2)
-        def _(slot):
-            for r in range(chunk):
-                row = slot * chunk + r
-                x = flat[pl.ds(row, n, stride=stride), :]
-                lanes = pl.ds(pl.multiple_of(row * nz, nz), nz)
-                for part, value in enumerate(limbs(x, anchor)):
-                    split_x[pl.ds(part * n, n), lanes] = value
-
-    def gram_of(begin, end, pair):
-        for slot in range(begin, end):
+        for at, count in ranges:
+
+            @pl.loop(at, at + count, unroll=2)
+            def _(slot):
+                for r in range(chunk):
+                    row = slot * chunk + r
+                    x = flat[pl.ds(row, n, stride=stride), :]
+                    lanes = pl.ds(pl.multiple_of(row * nz, nz), nz)
+                    for part, value in enumerate(limbs(x, anchor)):
+                        split_x[pl.ds(part * n, n), lanes] = value
+
+    def gram_of(ranges, pair):
+        for slot in (slot for at, count in ranges for slot in range(at, at + count)):
             x = split_x[:, slot * chunk * nz : (slot + 1) * chunk * nz]
             value = lax.dot_general(x, x, (((1,), (1,)), ((), ())), preferred_element_type=F32)
             if pair is None:
@@ -430,14 +426,14 @@
         full = jnp.dot(weights, split_x[:, lanes], preferred_element_type=F32)
         return full[0:n] + (full[n : 2 * n] + full[2 * n : 3 * n])
 
-    for a in range(own):
-        wait_cells(a, 0)
-    split_slots(0, half)
-    pair = gram_of(0, half, None)
-    for a in range(own):
-        wait_cells(a, 1)
-    split_slots(half, layers)
-    pair = gram_of(half, layers, pair)
+    pair = None
+    for part in range(3):
+        for a in range(own):
+            if part < len(pieces[a]) - 1:
+                wait_cells(a, part, fwd_recv)
+        ranges = slots_of[pieces[-1][part + 1]]
+        split_slots(ranges)
+        pair = gram_of(ranges, pair)
     gram = total(pair)
     weights = stacked(combined(gram, float(cells), n))
 
@@ -477,10 +473,10 @@
         pltpu.make_async_copy(block, block, bck_recv.at[part]).wait()
         single = back.at[pl.ds(0, own), pl.ds(at, count)]
         pltpu.make_async_copy(single, single, bck_own.at[part]).wait()
+    wait_margins(pot_send)
     for a in range(own):
-        for part, (at, count) in enumerate(((0, half), (half, 6))):
-            block = grouped.at[pl.ds(0, orbs - 1), pl.ds(at, count)]
-            pltpu.make_async_copy(block, block, fwd_send.at[a, part]).wait()
+        for part in range(len(pieces[a]) - 1):
+            wait_cells(a, part, fwd_send)
     for which, buf in enumerate((gram_orb, gram_dom)):
         block = buf.at[pl.ds(0, (orbs, doms)[which] - 1)]
         pltpu.make_async_copy(block, block, gram_send.at[which]).wait()
@@ -516,13 +512,12 @@
             pltpu.VMEM((orbs, 4, 128), F32),
             pltpu.VMEM((doms, 4, 128), F32),
             dma((1 + own,)),
-            dma((own, 3, 2)),
-            dma((own, 3, 2)),
+            dma((own, 4, 2)),
+            dma((own, 4, 2)),
             dma((2, 2)),
             dma((2, 2)),
-            dma((own, 2)),
-            dma((own, 2)),
-            dma((own, 2)),
+            dma((own, 3)),
+            dma((own, 3)),
             dma((2,)),
             dma((2,)),
             dma((3,)),

time: 62.5 us -> 59.6 us (0.954)
  Pallas kernels: 61.6 us -> 58.6 us
    pallas_call x1, Pallas kernels: 61.6 us -> 58.6 us  [on_device(): pl.pallas_call(functools.partial(kernel, (doms, orbs, own, layers, ny, nz...]
where the time goes in v4:
time: 59.6 us; the launch traced here: 59.5 us
  Pallas kernels  58.6 us (98%)
  local copies, waits for them, and re-layouts  0.88 us (1%)
    pallas_call x1, Pallas kernels, on_device(): pl.pallas_call(functools.partial(kernel, (doms, orbs, own, layers, ny, nz...  58.6 us

profile of v4, /device:TPU:1, one launch (start us, length us, event | category | flops | bytes accessed | tf_op | source)
XLA Modules:
  0.0 59.5 jit_solution(17958395283467440457)
XLA Ops:
  0.0 58.6 %shard_map.28 = f32[2,12,64,128]{3,2,1,0:T(8,128)S(1)} custom-call(f32[2,12,64,128]{3,2,1,0:T(8,128)} %orb_ref.1, f32[12,64,128]{2,1,0:T(8,128)} %pot_ref.1), custom_call_target="tpu_custom_call" | custom-call | flops 100000000 | bytes 4000000 | tf_op jit(solution)/shard_map/pallas_call | solution.py:497
  58.6 0.9 %copy.4 = f32[2,12,64,128]{3,2,1,0:T(8,128)} copy(f32[2,12,64,128]{3,2,1,0:T(8,128)S(1)} %shard_map.28) | data formatting | bytes 1572864

commit v5 on v4

--- a/solution.py
+++ b/solution.py
@@ -18,6 +18,7 @@
 STEP = tuple(kinetic * c for c in coefficients)
 DIAGONAL = 3.0 * STEP[0] - filter_centre / filter_half
 LIMBS = 4
+EARLY = 2
 
 
 def split3(x):
@@ -135,7 +136,11 @@
     raw,
     diag,
     third,
+    spread,
     grouped,
+    wide,
+    swap,
+    table,
     split_x,
     back,
     gram_orb,
@@ -151,12 +156,16 @@
     gram_recv,
     bck_send,
     bck_recv,
-    bck_own,
+    all_send,
+    all_recv,
+    swap_send,
+    swap_recv,
 ):
     doms, orbs, own, layers, ny, nz, cells = sizes
     n = own * orbs
     chunk = ny // orbs
     half = layers - 6
+    pairs = orbs // 2
     d = lax.axis_index("dom")
     o = lax.axis_index("orb")
     left = lax.rem(d + doms - 1, doms)
@@ -266,16 +275,23 @@
         if stage < 2:
             fields[stage + 1][a, at - 3] = result
         else:
-            third[:, a, (layer - 3) % layers] = result.reshape(orbs, chunk, nz)
+            tiles = result.reshape(orbs, chunk, nz)
+            slot = slot_layers.index(layer)
+            third[:, a, slot] = tiles
+            if slot < half:
+                for q in range(2 * pairs - 1):
+                    for parity in range(2):
+                        spread[parity, q, a, slot] = tiles[2 * (q % pairs) + parity]
 
     inner = range(3, layers - 3)
+    slot_layers = [*inner, 1, 2, layers - 3, layers - 2, 0, layers - 1]
 
     def newly(stage, a, begin, end):
         low, high = 3 * (stage + 1), layers - 3 * (stage + 1)
         for layer in (*range(low - end, low - begin), *range(high + begin, high + end)):
             apply_layer(stage, a, layer)
 
-    slots_of = {(3, 6): ((0, half),), (6, 9): ((half, 6),), (6, 8): ((half, 2), (half + 4, 2)), (8, 9): ((half + 2, 2),)}
+    slots_of = {(3, 6): ((0, half),), (6, 9): ((half, 6),), (6, 8): ((half, 4),), (8, 9): ((half + 4, 2),)}
 
     def to_cells(a, piece):
         part = pieces[a].index(piece) - 1
@@ -330,8 +346,43 @@
                 newly(2, a, begin, end)
                 to_cells(a, (begin, end))
 
+    place, parity = o // 2, lax.rem(o, 2)
+    other = o + 1 - 2 * parity
+
+    def gather(a, at, count):
+        @pl.loop(1, orbs)
+        def _(p):
+            to = lax.rem(o + p, orbs)
+            pltpu.make_async_remote_copy(
+                src_ref=spread.at[lax.rem(to, 2), pl.ds(to // 2 + 1, pairs - 1), a, pl.ds(at, count)],
+                dst_ref=wide.at[:, own * o + a, pl.ds(at, count)],
+                send_sem=all_send.at[0],
+                recv_sem=all_recv.at[0],
+                device_id={"orb": to},
+                device_id_type=MESH,
+            ).start()
+
+    def gather_own():
+        for k in range(1, pairs):
+            for a in range(own):
+                wide[k - 1, own * o + a] = spread[parity, place + k, a]
+
+    def gather_rest():
+        if EARLY < half:
+            gather(0, EARLY, half - EARLY)
+        for a in range(1, own):
+            gather(a, 0, half)
+        gather_own()
+
+    def gather_wait(sem):
+        block = wide.at[:, pl.ds(0, own * (orbs - 1))]
+        pltpu.make_async_copy(block, block, sem.at[0]).wait()
+
+    if EARLY:
+        gather(0, 0, EARLY)
+
     flat = grouped.reshape(n * layers * chunk, nz)
-    flat_back = back.reshape(n * layers * chunk, nz)
+    flat_back = back.reshape(n * 6 * chunk, nz)
     stride = layers * chunk
 
     def split_slots(ranges):
@@ -396,6 +447,8 @@
                     device_id_type=MESH,
                 ).start()
 
+            if which == 0:
+                gather_rest()
             block = buf.at[pl.ds(0, count - 1)]
             pltpu.make_async_copy(block, block, gram_recv.at[which]).wait()
             value, error = buf[...], None
@@ -435,14 +488,22 @@
         split_slots(ranges)
         pair = gram_of(ranges, pair)
     gram = total(pair)
-    weights = stacked(combined(gram, float(cells), n))
-
-    def send_back(part, at, count, layer):
+    matrix = combined(gram, float(cells), n)
+    weights = stacked(matrix)
+
+    parts = ((layers - 3, 3), (0, 3))
+    for part, (layer, count) in enumerate(parts):
+        for i in range(count):
+            slot = slot_layers.index(layer + i)
+            y = applied(weights, pl.ds(slot * chunk * nz, chunk * nz))
+            for r in range(chunk):
+                flat_back[pl.ds((part * 3 + i) * chunk + r, n, stride=6 * chunk), :] = y[:, r * nz : (r + 1) * nz]
+
         @pl.loop(1, orbs)
         def _(p):
             to = lax.rem(o + p, orbs)
             pltpu.make_async_remote_copy(
-                src_ref=back.at[pl.ds(own * to, own), pl.ds(at, count)],
+                src_ref=back.at[pl.ds(own * to, own), pl.ds(part * 3, count)],
                 dst_ref=out_ref.at[:, pl.ds(layer, count), pl.ds(chunk * o, chunk)],
                 send_sem=bck_send.at[part],
                 recv_sem=bck_recv.at[part],
@@ -450,29 +511,52 @@
                 device_id_type=MESH,
             ).start()
 
-        pltpu.make_async_copy(
-            back.at[pl.ds(own * o, own), pl.ds(at, count)],
-            out_ref.at[:, pl.ds(layer, count), pl.ds(chunk * o, chunk)],
-            bck_own.at[part],
+    all_rows = lax.broadcasted_iota(jnp.int32, (n, 128), 0)
+    for i in range(2 * own):
+        chosen = own * o + i if i < own else own * other + i - own
+        row = jnp.sum(jnp.where(all_rows == chosen, matrix, 0.0), axis=0, keepdims=True)
+        row = jnp.broadcast_to(row, (8, 128))
+        for j in range(n):
+            table[i, j] = lane_of(row, j)
+    gather_wait(all_recv)
+
+    def chunk_rows(k):
+        return pl.ds(pl.multiple_of(chunk * (2 * lax.rem(place + k, pairs) + parity), chunk), chunk)
+
+    @pl.loop(0, half)
+    def _(slot):
+        for k in range(pairs):
+            x = [grouped[j, slot] if k == 0 else wide[k - 1, j, slot] for j in range(n)]
+            for i in range(2 * own):
+                terms = [table[i, j] * x[j] for j in range(n)]
+                while len(terms) > 1:
+                    terms = [p + q for p, q in zip(terms[::2], terms[1::2])]
+                if i < own:
+                    out_ref[i, slot + 3, chunk_rows(k), :] = terms[0]
+                else:
+                    swap[k, i - own, slot] = terms[0]
+
+    for k in range(pairs):
+        pltpu.make_async_remote_copy(
+            src_ref=swap.at[k],
+            dst_ref=out_ref.at[:, pl.ds(3, half), chunk_rows(k)],
+            send_sem=swap_send.at[0],
+            recv_sem=swap_recv.at[0],
+            device_id={"orb": other},
+            device_id_type=MESH,
         ).start()
-
-    parts = ((0, half, 3), (half, 3, half + 3), (half + 3, 3, 0))
-    for part, (at, count, layer) in enumerate(parts):
-
-        @pl.loop(at, at + count)
-        def _(slot):
-            lanes = pl.ds(pl.multiple_of(slot * chunk * nz, chunk * nz), chunk * nz)
-            y = applied(weights, lanes)
-            for r in range(chunk):
-                flat_back[pl.ds(slot * chunk + r, n, stride=stride), :] = y[:, r * nz : (r + 1) * nz]
-
-        send_back(part, at, count, layer)
-    for part, (at, count, layer) in enumerate(parts):
-        block = back.at[pl.ds(0, own * (orbs - 1)), pl.ds(at, count)]
+    for a in range(own):
+        for part, (layer, count) in enumerate(parts):
+            out_ref[a, pl.ds(layer, count), pl.ds(pl.multiple_of(chunk * o, chunk), chunk), :] = back[
+                own * o + a, pl.ds(part * 3, count)
+            ]
+    for sem in (swap_send, swap_recv):
+        pltpu.make_async_copy(swap, swap, sem.at[0]).wait()
+    for part, (layer, count) in enumerate(parts):
+        block = back.at[pl.ds(0, own * (orbs - 1)), pl.ds(part * 3, count)]
         pltpu.make_async_copy(block, block, bck_send.at[part]).wait()
         pltpu.make_async_copy(block, block, bck_recv.at[part]).wait()
-        single = back.at[pl.ds(0, own), pl.ds(at, count)]
-        pltpu.make_async_copy(single, single, bck_own.at[part]).wait()
+    gather_wait(all_send)
     wait_margins(pot_send)
     for a in range(own):
         for part in range(len(pieces[a]) - 1):
@@ -506,9 +590,13 @@
             pltpu.VMEM((layers + 12, ny, nz), F32),
             pltpu.VMEM((layers + 12, ny, nz), F32),
             pltpu.VMEM((orbs, own, layers, chunk, nz), F32),
+            pltpu.VMEM((2, orbs - 1, own, layers - 6, chunk, nz), F32),
             pltpu.VMEM((n, layers, chunk, nz), F32),
+            pltpu.VMEM((orbs // 2 - 1, n, layers - 6, chunk, nz), F32),
+            pltpu.VMEM((orbs // 2, own, layers - 6, chunk, nz), F32),
+            pltpu.VMEM((2 * own, n, 8, 128), F32),
             pltpu.VMEM((LIMBS * n, width), BF16),
-            pltpu.VMEM((n, layers, chunk, nz), F32),
+            pltpu.VMEM((n, 6, chunk, nz), F32),
             pltpu.VMEM((orbs, 4, 128), F32),
             pltpu.VMEM((doms, 4, 128), F32),
             dma((1 + own,)),
@@ -520,9 +608,12 @@
             dma((own, 3)),
             dma((2,)),
             dma((2,)),
-            dma((3,)),
-            dma((3,)),
-            dma((3,)),
+            dma((2,)),
+            dma((2,)),
+            dma((1,)),
+            dma((1,)),
+            dma((1,)),
+            dma((1,)),
         ],
         compiler_params=pltpu.CompilerParams(
             collective_id=0, has_side_effects=True, vmem_limit_bytes=40 * 1024 * 1024

time: 59.6 us -> 56 us (0.940)
  Pallas kernels: 58.6 us -> 55 us
    pallas_call x1, Pallas kernels: 58.6 us -> 55 us  [on_device(): pl.pallas_call(functools.partial(kernel, (doms, orbs, own, layers, ny, nz...]
where the time goes in v5:
time: 56 us; the launch traced here: 55.9 us
  Pallas kernels  55 us (98%)
  local copies, waits for them, and re-layouts  0.88 us (2%)
    pallas_call x1, Pallas kernels, on_device(): pl.pallas_call(functools.partial(kernel, (doms, orbs, own, layers, ny, nz...  55 us

profile of v5, /device:TPU:1, one launch (start us, length us, event | category | flops | bytes accessed | tf_op | source)
XLA Modules:
  0.0 55.9 jit_solution(17302020998145556572)
XLA Ops:
  0.0 55.0 %shard_map.28 = f32[2,12,64,128]{3,2,1,0:T(8,128)S(1)} custom-call(f32[2,12,64,128]{3,2,1,0:T(8,128)} %orb_ref.1, f32[12,64,128]{2,1,0:T(8,128)} %pot_ref.1), custom_call_target="tpu_custom_call" | custom-call | flops 100000000 | bytes 4000000 | tf_op jit(solution)/shard_map/pallas_call | solution.py:581
  55.0 0.9 %copy.4 = f32[2,12,64,128]{3,2,1,0:T(8,128)} copy(f32[2,12,64,128]{3,2,1,0:T(8,128)S(1)} %shard_map.28) | data formatting | bytes 1572864

commit v6 on v5

--- a/solution.py
+++ b/solution.py
@@ -18,7 +18,7 @@
 STEP = tuple(kinetic * c for c in coefficients)
 DIAGONAL = 3.0 * STEP[0] - filter_centre / filter_half
 LIMBS = 4
-EARLY = 2
+GATHERED = 6
 
 
 def split3(x):
@@ -278,7 +278,7 @@
             tiles = result.reshape(orbs, chunk, nz)
             slot = slot_layers.index(layer)
             third[:, a, slot] = tiles
-            if slot < half:
+            if slot < GATHERED:
                 for q in range(2 * pairs - 1):
                     for parity in range(2):
                         spread[parity, q, a, slot] = tiles[2 * (q % pairs) + parity]
@@ -299,7 +299,7 @@
 
             @pl.loop(1, orbs)
             def _(p):
-                to = lax.rem(o + p, orbs)
+                to = lax.rem(o + 1 + lax.rem(p + 2, orbs - 1), orbs)
                 pltpu.make_async_remote_copy(
                     src_ref=third.at[to, a, pl.ds(at, count)],
                     dst_ref=grouped.at[own * o + a, pl.ds(at, count)],
@@ -349,13 +349,13 @@
     place, parity = o // 2, lax.rem(o, 2)
     other = o + 1 - 2 * parity
 
-    def gather(a, at, count):
+    def gather(a):
         @pl.loop(1, orbs)
         def _(p):
-            to = lax.rem(o + p, orbs)
+            to = lax.rem(o + 1 + lax.rem(p + 2, orbs - 1), orbs)
             pltpu.make_async_remote_copy(
-                src_ref=spread.at[lax.rem(to, 2), pl.ds(to // 2 + 1, pairs - 1), a, pl.ds(at, count)],
-                dst_ref=wide.at[:, own * o + a, pl.ds(at, count)],
+                src_ref=spread.at[lax.rem(to, 2), pl.ds(to // 2 + 1, pairs - 1), a],
+                dst_ref=wide.at[:, own * o + a],
                 send_sem=all_send.at[0],
                 recv_sem=all_recv.at[0],
                 device_id={"orb": to},
@@ -368,21 +368,16 @@
                 wide[k - 1, own * o + a] = spread[parity, place + k, a]
 
     def gather_rest():
-        if EARLY < half:
-            gather(0, EARLY, half - EARLY)
-        for a in range(1, own):
-            gather(a, 0, half)
+        for a in range(own):
+            gather(a)
         gather_own()
 
     def gather_wait(sem):
         block = wide.at[:, pl.ds(0, own * (orbs - 1))]
         pltpu.make_async_copy(block, block, sem.at[0]).wait()
 
-    if EARLY:
-        gather(0, 0, EARLY)
-
     flat = grouped.reshape(n * layers * chunk, nz)
-    flat_back = back.reshape(n * 6 * chunk, nz)
+    flat_back = back.reshape(n * (layers - GATHERED) * chunk, nz)
     stride = layers * chunk
 
     def split_slots(ranges):
@@ -443,7 +438,7 @@
                     dst_ref=buf.at[me],
                     send_sem=gram_send.at[which],
                     recv_sem=gram_recv.at[which],
-                    device_id={axis: lax.rem(me + p, count)},
+                    device_id={axis: lax.rem(me + 1 + lax.rem(p + count // 2 - 2, count - 1), count)},
                     device_id_type=MESH,
                 ).start()
 
@@ -491,19 +486,19 @@
     matrix = combined(gram, float(cells), n)
     weights = stacked(matrix)
 
-    parts = ((layers - 3, 3), (0, 3))
-    for part, (layer, count) in enumerate(parts):
+    parts = ((3 + GATHERED, layers - 3 - GATHERED, 0), (0, 3, layers - 3 - GATHERED))
+    for part, (layer, count, at) in enumerate(parts):
         for i in range(count):
             slot = slot_layers.index(layer + i)
             y = applied(weights, pl.ds(slot * chunk * nz, chunk * nz))
             for r in range(chunk):
-                flat_back[pl.ds((part * 3 + i) * chunk + r, n, stride=6 * chunk), :] = y[:, r * nz : (r + 1) * nz]
+                flat_back[pl.ds((at + i) * chunk + r, n, stride=(layers - GATHERED) * chunk), :] = y[:, r * nz : (r + 1) * nz]
 
         @pl.loop(1, orbs)
         def _(p):
-            to = lax.rem(o + p, orbs)
+            to = lax.rem(o + 1 + lax.rem(p + 2, orbs - 1), orbs)
             pltpu.make_async_remote_copy(
-                src_ref=back.at[pl.ds(own * to, own), pl.ds(part * 3, count)],
+                src_ref=back.at[pl.ds(own * to, own), pl.ds(at, count)],
                 dst_ref=out_ref.at[:, pl.ds(layer, count), pl.ds(chunk * o, chunk)],
                 send_sem=bck_send.at[part],
                 recv_sem=bck_recv.at[part],
@@ -523,7 +518,7 @@
     def chunk_rows(k):
         return pl.ds(pl.multiple_of(chunk * (2 * lax.rem(place + k, pairs) + parity), chunk), chunk)
 
-    @pl.loop(0, half)
+    @pl.loop(0, GATHERED)
     def _(slot):
         for k in range(pairs):
             x = [grouped[j, slot] if k == 0 else wide[k - 1, j, slot] for j in range(n)]
@@ -539,21 +534,21 @@
     for k in range(pairs):
         pltpu.make_async_remote_copy(
             src_ref=swap.at[k],
-            dst_ref=out_ref.at[:, pl.ds(3, half), chunk_rows(k)],
+            dst_ref=out_ref.at[:, pl.ds(3, GATHERED), chunk_rows(k)],
             send_sem=swap_send.at[0],
             recv_sem=swap_recv.at[0],
             device_id={"orb": other},
             device_id_type=MESH,
         ).start()
     for a in range(own):
-        for part, (layer, count) in enumerate(parts):
+        for layer, count, at in parts:
             out_ref[a, pl.ds(layer, count), pl.ds(pl.multiple_of(chunk * o, chunk), chunk), :] = back[
-                own * o + a, pl.ds(part * 3, count)
+                own * o + a, pl.ds(at, count)
             ]
     for sem in (swap_send, swap_recv):
         pltpu.make_async_copy(swap, swap, sem.at[0]).wait()
-    for part, (layer, count) in enumerate(parts):
-        block = back.at[pl.ds(0, own * (orbs - 1)), pl.ds(part * 3, count)]
+    for part, (_, count, at) in enumerate(parts):
+        block = back.at[pl.ds(0, own * (orbs - 1)), pl.ds(at, count)]
         pltpu.make_async_copy(block, block, bck_send.at[part]).wait()
         pltpu.make_async_copy(block, block, bck_recv.at[part]).wait()
     gather_wait(all_send)
@@ -590,13 +585,13 @@
             pltpu.VMEM((layers + 12, ny, nz), F32),
             pltpu.VMEM((layers + 12, ny, nz), F32),
             pltpu.VMEM((orbs, own, layers, chunk, nz), F32),
-            pltpu.VMEM((2, orbs - 1, own, layers - 6, chunk, nz), F32),
+            pltpu.VMEM((2, orbs - 1, own, GATHERED, chunk, nz), F32),
             pltpu.VMEM((n, layers, chunk, nz), F32),
-            pltpu.VMEM((orbs // 2 - 1, n, layers - 6, chunk, nz), F32),
-            pltpu.VMEM((orbs // 2, own, layers - 6, chunk, nz), F32),
+            pltpu.VMEM((orbs // 2 - 1, n, GATHERED, chunk, nz), F32),
+            pltpu.VMEM((orbs // 2, own, GATHERED, chunk, nz), F32),
             pltpu.VMEM((2 * own, n, 8, 128), F32),
             pltpu.VMEM((LIMBS * n, width), BF16),
-            pltpu.VMEM((n, 6, chunk, nz), F32),
+            pltpu.VMEM((n, layers - GATHERED, chunk, nz), F32),
             pltpu.VMEM((orbs, 4, 128), F32),
             pltpu.VMEM((doms, 4, 128), F32),
             dma((1 + own,)),

time: 56 us -> 55.1 us (0.984)
  Pallas kernels: 55 us -> 54.1 us
    pallas_call x1, Pallas kernels: 55 us -> 54.1 us  [on_device(): pl.pallas_call(functools.partial(kernel, (doms, orbs, own, layers, ny, nz...]
where the time goes in v6:
time: 55.1 us; the launch traced here: 55 us
  Pallas kernels  54.1 us (98%)
  local copies, waits for them, and re-layouts  0.88 us (2%)
    pallas_call x1, Pallas kernels, on_device(): pl.pallas_call(functools.partial(kernel, (doms, orbs, own, layers, ny, nz...  54.1 us

profile of v6, /device:TPU:1, one launch (start us, length us, event | category | flops | bytes accessed | tf_op | source)
XLA Modules:
  0.0 55.0 jit_solution(14896004442387568651)
XLA Ops:
  0.0 54.1 %shard_map.28 = f32[2,12,64,128]{3,2,1,0:T(8,128)S(1)} custom-call(f32[2,12,64,128]{3,2,1,0:T(8,128)} %orb_ref.1, f32[12,64,128]{2,1,0:T(8,128)} %pot_ref.1), custom_call_target="tpu_custom_call" | custom-call | flops 100000000 | bytes 4000000 | tf_op jit(solution)/shard_map/pallas_call | solution.py:576
  54.1 0.9 %copy.4 = f32[2,12,64,128]{3,2,1,0:T(8,128)} copy(f32[2,12,64,128]{3,2,1,0:T(8,128)S(1)} %shard_map.28) | data formatting | bytes 1572864

commit v7 on v6

--- a/solution.py
+++ b/solution.py
@@ -173,17 +173,27 @@
 
     barrier = pltpu.get_barrier_semaphore()
 
-    @pl.loop(1, orbs)
+    near, far = 2 * orbs, doms // 2
+    parity_d = lax.rem(d, 2)
+    place_near = parity_d * orbs + o
+
+    def near_device(p):
+        to = lax.rem(place_near + p, near)
+        return {"dom": d - parity_d + to // orbs, "orb": lax.rem(to, orbs)}
+
+    def far_device(p):
+        return {"dom": 2 * lax.rem(d // 2 + p, far) + parity_d}
+
+    for neighbour in (left, right):
+        pl.semaphore_signal(barrier, inc=1, device_id={"dom": neighbour}, device_id_type=MESH)
+
+    @pl.loop(1, far)
     def _(p):
-        pl.semaphore_signal(
-            barrier, inc=1, device_id={"orb": lax.rem(o + p, orbs)}, device_id_type=MESH
-        )
-
-    @pl.loop(1, doms)
+        pl.semaphore_signal(barrier, inc=1, device_id=far_device(p), device_id_type=MESH)
+
+    @pl.loop(1, near)
     def _(p):
-        pl.semaphore_signal(
-            barrier, inc=1, device_id={"dom": lax.rem(d + p, doms)}, device_id_type=MESH
-        )
+        pl.semaphore_signal(barrier, inc=1, device_id=near_device(p), device_id_type=MESH)
 
     loads = [pltpu.make_async_copy(pot_ref, raw.at[pl.ds(6, layers)], load_sem.at[0])]
     for a in range(own):
@@ -191,7 +201,7 @@
     for copy in loads:
         copy.start()
 
-    pl.semaphore_wait(barrier, orbs - 1 + doms - 1)
+    pl.semaphore_wait(barrier, 2 + near - 1 + far - 1)
 
     fields = (e0, e1, e2)
 
@@ -428,7 +438,9 @@
         high, low = (jnp.where(lane < n, t, b) for t, b in zip(top, bottom))
         packed = jnp.where(lane < 2 * n, high, pltpu.roll(low, 2 * n, 1))
         packed = jnp.where(lane4 < 64, packed[:4], pltpu.roll(packed, 64, 1)[4:])
-        for which, (axis, count, me, buf) in enumerate((("orb", orbs, o, gram_orb), ("dom", doms, d, gram_dom))):
+        for which, (target, count, me, buf) in enumerate(
+            ((near_device, near, place_near, gram_orb), (far_device, far, d // 2, gram_dom))
+        ):
             buf[me] = packed
 
             @pl.loop(1, count)
@@ -438,7 +450,7 @@
                     dst_ref=buf.at[me],
                     send_sem=gram_send.at[which],
                     recv_sem=gram_recv.at[which],
-                    device_id={axis: lax.rem(me + 1 + lax.rem(p + count // 2 - 2, count - 1), count)},
+                    device_id=target(1 + lax.rem(p + count // 2 - 2, count - 1)),
                     device_id_type=MESH,
                 ).start()
 
@@ -557,7 +569,7 @@
         for part in range(len(pieces[a]) - 1):
             wait_cells(a, part, fwd_send)
     for which, buf in enumerate((gram_orb, gram_dom)):
-        block = buf.at[pl.ds(0, (orbs, doms)[which] - 1)]
+        block = buf.at[pl.ds(0, (near, far)[which] - 1)]
         pltpu.make_async_copy(block, block, gram_send.at[which]).wait()
 
 
@@ -592,8 +604,8 @@
             pltpu.VMEM((2 * own, n, 8, 128), F32),
             pltpu.VMEM((LIMBS * n, width), BF16),
             pltpu.VMEM((n, layers - GATHERED, chunk, nz), F32),
-            pltpu.VMEM((orbs, 4, 128), F32),
-            pltpu.VMEM((doms, 4, 128), F32),
+            pltpu.VMEM((2 * orbs, 4, 128), F32),
+            pltpu.VMEM((doms // 2, 4, 128), F32),
             dma((1 + own,)),
             dma((own, 4, 2)),
             dma((own, 4, 2)),

time: 55.1 us -> 55.4 us (level)
  no operation moved by 1% of the time
where the time goes in v7:
time: 55.4 us
  Pallas kernels  54.5 us (98%)
  local copies, waits for them, and re-layouts  0.88 us (2%)
    pallas_call x1, Pallas kernels, on_device(): pl.pallas_call(functools.partial(kernel, (doms, orbs, own, layers, ny, nz...  54.5 us

profile of v7, /device:TPU:1, one launch (start us, length us, event | category | flops | bytes accessed | tf_op | source)
XLA Modules:
  0.0 55.4 jit_solution(1344647352880391235)
XLA Ops:
  0.0 54.5 %shard_map.28 = f32[2,12,64,128]{3,2,1,0:T(8,128)S(1)} custom-call(f32[2,12,64,128]{3,2,1,0:T(8,128)} %orb_ref.1, f32[12,64,128]{2,1,0:T(8,128)} %pot_ref.1), custom_call_target="tpu_custom_call" | custom-call | flops 100000000 | bytes 4000000 | tf_op jit(solution)/shard_map/pallas_call | solution.py:588
  54.5 0.9 %copy.4 = f32[2,12,64,128]{3,2,1,0:T(8,128)} copy(f32[2,12,64,128]{3,2,1,0:T(8,128)S(1)} %shard_map.28) | data formatting | bytes 1572864
